TPU v7x, 256 devices: a whole 4x4x8 slice. The times are simulated.
256 devices in a mesh: scan: 8 (over x, y_hi), tile: 32 (over y_lo, z, core).
Axes of the slice: x: 4, y: 4 (y_hi: 2, y_lo: 2; y = y_hi * 2 + y_lo), z: 8, core: 2. Of those that a mesh axis runs over, the one named last changes fastest.
Arguments:
- object_field: float32 [2, 8192, 512], P(None, 'tile'), may hold values from -6 to 6
- probe: float32 [2, 256, 256], replicated, may hold values from -18 to 18
- amplitudes: bfloat16 [8, 32, 12, 256, 256], P('scan', 'tile'), may hold values from 0 to 6
- positions: int32 [8, 32, 12, 2], P('scan', 'tile'), may hold values from 0 to 7936, as said below
- counts: int32 [8, 32], P('scan', 'tile'), may hold values from 1 to 12, as said below
Outputs:
- new_object: float32 [2, 8192, 512], P(None, 'tile')
- new_probe: float32 [2, 256, 256], replicated
- probe_gradient: float32 [2, 256, 256], replicated
Inputs may be any that keep to these rules, and one draw needn't show every extreme that they name: `positions`: every slot of the device at tile t names a window whose first row lies in rows t * 256 to (t + 1) * 256 - 1 and is at most 7936, and whose first column is at most 256; both ends are reached. `counts`: slots at and beyond a device's count are ignored; some device has exactly 12 live slots.
All inputs are finite; a program needn't handle non-finite values.
Results may differ from a plain program's by a relative error of at most 0.0065.
Values may be sent and summed in bfloat16 or wider, within the bound.
No kernel may reach another device: no remote copies, remote signals or barrier semaphores. Data moves between devices by JAX's collectives and lax.ppermute only.
A program may use at most 64 MiB of HBM per device.

v0:
```python
import functools
import math

import jax
import jax.numpy as jnp
import numpy as np
from jax import lax
from jax.experimental import pallas as pl
from jax.experimental.pallas import tpu as pltpu
from jax.sharding import PartitionSpec as P

ITERS = 2
PS = 256
TH = 256
OW = 512
CAP = 12
NS = 8
NT = 32
SR = TH // NS
LN = 128
GRANT = 20
SOME = 4
UN = 8
PAIR = 3
FLOOR2 = 0.25
REG = 1.0

OWN, NEXT, PRB, POS = 0, 2 * SR, 4 * SR, 4 * SR + 48
SEND = POS + 16
GROUP = 12

BF = jnp.bfloat16
F32 = jnp.float32


def tables():
    n = np.arange(PS, dtype=np.int64)
    angle = ((n[:, None] * n[None, :]) % PS).astype(np.float32) * np.float32(2.0 * math.pi / PS)
    c = (np.cos(angle) / np.sqrt(PS)).astype(np.float32)
    s = (np.sin(angle) / np.sqrt(PS)).astype(np.float32)
    return c, s


def table_arrays():
    return [jnp.asarray(t.astype(jnp.bfloat16)) for t in tables()]


def prepare_kernel(c_ref, s_ref, amp_ref, amp_out, m1_ref, m2_ref, sems):
    copies = [pltpu.make_async_copy(amp_ref.at[j], amp_out.at[j], sems.at[j]) for j in range(CAP)]
    for copy in copies:
        copy.start()
    c = c_ref[...]
    s = s_ref[...]
    for table, upper, lower in ((m1_ref, -s, s), (m2_ref, s, -s)):
        table[:PS, :PS] = c
        table[:PS, PS:] = upper
        table[PS:, :PS] = lower
        table[PS:, PS:] = c
    for copy in copies:
        copy.wait()


def prepare(amps):
    table = jax.ShapeDtypeStruct((2 * PS, 2 * PS), BF)
    return pl.pallas_call(
        prepare_kernel,
        out_shape=[jax.ShapeDtypeStruct(amps.shape, BF), table, table],
        in_specs=[vmem(), vmem(), pl.BlockSpec(memory_space=pltpu.HBM)],
        out_specs=[vmem()] * 3,
        scratch_shapes=[pltpu.SemaphoreType.DMA((CAP,))],
        compiler_params=params(8),
        cost_estimate=pl.CostEstimate(flops=0, bytes_accessed=8 << 20, transcendentals=0),
        name="prepare",
    )(*table_arrays(), amps)


def pattern_kernel(first, pos_ref, cnt_ref, obj_ref, halo_ref, probe_ref, amp_ref, extra_ref, m1, m2, *rest):
    if first:
        send, x, g, pg, patch, h, h2 = rest
        pr = probe_ref
    else:
        send, objn_ref, pr, x, g, pg, patch, h, h2 = rest
    count = cnt_ref[0]
    lane_blocks = [slice(q * LN, (q + 1) * LN) for q in range(4)]
    tile_start = lax.axis_index("tile") * TH
    g[...] = jnp.zeros_like(g)
    pg[...] = jnp.zeros_like(pg)
    if first:
        for q in range(4):
            x[:, q, :TH, :] = obj_ref[:, :, lane_blocks[q]]
            x[:, q, TH:, :] = halo_ref[:, :, lane_blocks[q]].astype(F32)
    else:
        for s in range(NS):
            for k in range(2):
                a = s * SR
                d = obj_ref[k, a : a + SR, :] + extra_ref[s, k * SR : (k + 1) * SR, :].astype(F32)
                e = halo_ref[k, a : a + SR, :].astype(F32) + extra_ref[s, (2 + k) * SR : (3 + k) * SR, :].astype(F32)
                objn_ref[k, a : a + SR, :] = d
                for q in range(4):
                    x[k, q, a : a + SR, :] = d[:, lane_blocks[q]]
                    x[k, q, TH + a : TH + a + SR, :] = e[:, lane_blocks[q]]
                d = extra_ref[s, 4 * SR + 16 * k : 4 * SR + 16 * (k + 1), :].astype(F32)
                for q in range(2):
                    b = a + 16 * q
                    pr[k, b : b + 16, :] = probe_ref[k, b : b + 16, :] + d[:, q * PS : (q + 1) * PS]

    def place(j):
        r = pos_ref[0, j] - tile_start
        c = pos_ref[1, j]
        base = jnp.where(c >= LN, 1, 0)
        return r, base, c - base * LN

    lanes = lax.broadcasted_iota(jnp.int32, (PS, LN), 1)

    def to_half(j, slot, live):
        r, base, off = place(j)
        head = lanes < LN - off
        turn = (LN - off) & (LN - 1)
        xs = []
        for k in range(2):
            v = [pltpu.roll(x[k, base + q, pl.ds(r, PS), :], turn, 1) for q in range(3)]
            v = jnp.concatenate([jnp.where(head, v[0], v[1]), jnp.where(head, v[1], v[2])], 1)
            patch[slot, k] = v
            xs.append(v)
        xr, xi = xs
        p0, p1 = pr[0], pr[1]
        pg[2] += (xr * xr + xi * xi) * live
        return jnp.concatenate([(p0 * xr - p1 * xi).astype(BF), (p0 * xi + p1 * xr).astype(BF)], 1)

    def half_dot(w, slot):
        for b in range(2):
            half = jnp.dot(w, m1[:, b * PS : (b + 1) * PS], preferred_element_type=F32)
            h[slot, b * PS : (b + 1) * PS, :] = half.astype(BF)

    def far_dot(slot):
        fr = jnp.dot(m2[:PS, :], h[slot], preferred_element_type=F32)
        fi = jnp.dot(m2[PS:, :], h[slot], preferred_element_type=F32)
        return fr, fi

    def update(j, live, far):
        fr, fi = far
        m = jnp.maximum(fr * fr + fi * fi, FLOOR2)
        q = amp_ref[j].astype(F32) * lax.rsqrt(m) - 1.0
        q = q * live
        return jnp.concatenate([(q * fr).astype(BF), (q * fi).astype(BF)], 1)

    def back_half_dot(u, slot):
        for b in range(2):
            half = jnp.dot(u, m2[:, b * PS : (b + 1) * PS], preferred_element_type=F32)
            h2[slot, b * PS : (b + 1) * PS, :] = half.astype(BF)

    def back_dot(slot):
        br = jnp.dot(m1[:PS, :], h2[slot], preferred_element_type=F32)
        bi = jnp.dot(m1[PS:, :], h2[slot], preferred_element_type=F32)
        return br, bi

    def add_back(j, slot, back):
        br, bi = back
        xr, xi = patch[slot, 0], patch[slot, 1]
        pg[0] += xr * br + xi * bi
        pg[1] += xr * bi - xi * br
        p0, p1 = pr[0], pr[1]
        r, base, off = place(j)
        tail = lanes >= off
        turn = off & (LN - 1)
        for k, o in enumerate((p0 * br + p1 * bi, p0 * bi - p1 * br)):
            v = [pltpu.roll(o[:, q * LN : (q + 1) * LN], turn, 1) for q in range(2)]
            g[k, base, pl.ds(r, PS), :] += jnp.where(tail, v[0], 0.0)
            g[k, base + 1, pl.ds(r, PS), :] += jnp.where(tail, v[1], v[0])
            g[k, base + 2, pl.ds(r, PS), :] += jnp.where(tail, 0.0, v[1])

    def visit(i, carry):
        j = [PAIR * i + n for n in range(PAIR)]
        live = [jnp.where(n < count, 1.0, 0.0) for n in j]
        w = to_half(j[0], 0, live[0])
        for n in range(PAIR):
            half_dot(w, n)
            if n + 1 < PAIR:
                w = to_half(j[n + 1], n + 1, live[n + 1])
        fars = [far_dot(n) for n in range(PAIR)]
        us = [update(j[n], live[n], fars[n]) for n in range(PAIR)]
        for n in range(PAIR):
            back_half_dot(us[n], n)
        backs = [back_dot(n) for n in range(PAIR)]
        for n in range(PAIR):
            add_back(j[n], n, backs[n])
        return carry

    lax.fori_loop(0, jnp.minimum((count + PAIR - 1) // PAIR, CAP // PAIR), visit, 0)
    for s in range(NS):
        a = s * SR
        for k in range(2):
            for q in range(4):
                send[s, OWN + k * SR : OWN + (k + 1) * SR, lane_blocks[q]] = g[k, q, a : a + SR, :].astype(BF)
                send[s, NEXT + k * SR : NEXT + (k + 1) * SR, lane_blocks[q]] = g[k, q, TH + a : TH + a + SR, :].astype(BF)
        for k in range(3):
            send[s, PRB + 16 * k : PRB + 16 * (k + 1), :] = jnp.concatenate(
                [pg[k, a : a + 16, :], pg[k, a + 16 : a + 32, :]], 1
            ).astype(BF)
        if first:
            send[s, POS:, :] = extra_ref[...]


def smem():
    return pl.BlockSpec(memory_space=pltpu.SMEM)


def vmem():
    return pl.BlockSpec(memory_space=pltpu.VMEM)


def params(mib):
    return pltpu.CompilerParams(vmem_limit_bytes=mib * 1024 * 1024)


def patterns(pos, cnt, obj, halo, probe, amps, tabs, posblk=None, recv=None):
    first = recv is None
    out = [jax.ShapeDtypeStruct((NS, SEND if first else POS, OW), BF)]
    if not first:
        out += [jax.ShapeDtypeStruct((2, TH, OW), F32), jax.ShapeDtypeStruct((2, PS, PS), F32)]
    args = [pos, cnt, obj, halo, probe, amps, posblk if first else recv, *tabs]
    return pl.pallas_call(
        functools.partial(pattern_kernel, first),
        out_shape=out,
        in_specs=[smem(), smem()] + [vmem()] * 7,
        out_specs=[vmem()] * len(out),
        scratch_shapes=[
            pltpu.VMEM((2, 4, 2 * TH, LN), F32),
            pltpu.VMEM((2, 4, 2 * TH, LN), F32),
            pltpu.VMEM((3, PS, PS), F32),
            pltpu.VMEM((PAIR, 2, PS, PS), F32),
            pltpu.VMEM((PAIR, 2 * PS, PS), BF),
            pltpu.VMEM((PAIR, 2 * PS, PS), BF),
        ],
        compiler_params=params(GRANT),
        name="patterns",
    )(*args)


def sum_kernel(last, recv_ref, own_ref, probe_ref, up_ref, *rest):
    def total(a, n):
        t = [recv_ref[s, a : a + n, :].astype(F32) for s in range(NS)]
        return ((t[0] + t[1]) + (t[2] + t[3])) + ((t[4] + t[5]) + (t[6] + t[7]))

    probe_ref[...] = total(PRB, 48).astype(BF)
    own_ref[...] = total(OWN, 2 * SR)
    up_ref[: 2 * SR, :] = total(NEXT, 2 * SR).astype(BF)
    if not last:
        pos = total(POS, 16)
        rest[0][...] = pos[:, :LN]
        up_ref[2 * SR :, :] = pos.astype(BF)


def sums(last, recv):
    out = [jax.ShapeDtypeStruct((2 * SR, OW), F32), jax.ShapeDtypeStruct((48, OW), BF)]
    if last:
        out += [jax.ShapeDtypeStruct((2 * SR, OW), BF)]
    else:
        out += [jax.ShapeDtypeStruct((2 * SR + 16, OW), BF), jax.ShapeDtypeStruct((16, LN), F32)]
    return pl.pallas_call(
        functools.partial(sum_kernel, last),
        out_shape=out,
        in_specs=[vmem()],
        out_specs=[vmem()] * len(out),
        compiler_params=params(8),
        name="sums",
    )(recv)


def own_kernel(pos_ref, probe_ref, own_ref, up_ref, out_ref, p2, list_ref):
    for q in range(2):
        cols = slice(q * LN, (q + 1) * LN)
        p2[q, :SR, :] = jnp.zeros((SR, LN), F32)
        p2[q, SR + PS :, :] = jnp.zeros((SR, LN), F32)
        p2[q, SR : SR + PS, :] = probe_ref[0, :, cols] * probe_ref[0, :, cols] + probe_ref[1, :, cols] * probe_ref[1, :, cols]
    mine = lax.axis_index("scan") * SR + SR + 1
    lanes = lax.broadcasted_iota(jnp.int32, (8, LN), 1)
    parts = SR // 8

    def group(row, at):
        shift = mine + jnp.where(row < NS, TH, 0)

        def some(i, at):
            for n in range(SOME):
                code = pos_ref[row, SOME * i + n]
                start = shift - code
                list_ref[0, at] = start
                list_ref[1, at] = pos_ref[row, GROUP + SOME * i + n]
                at = at + jnp.where((start > 0) & (start < PS + SR) & (code > 0), 1, 0)
            return at

        return lax.fori_loop(0, (pos_ref[row, 2 * GROUP] + SOME - 1) // SOME, some, at)

    listed = lax.fori_loop(0, 2 * NS, group, 0)
    for n in range(UN):
        list_ref[0, listed + n] = 0
        list_ref[1, listed + n] = 0

    def some(i, carry):
        carry = [list(c) for c in carry]
        for n in range(UN):
            at = list_ref[0, UN * i + n]
            c = list_ref[1, UN * i + n]
            far = c >= LN
            off = jnp.where(far, c - LN, c)
            tail = lanes >= off
            turn = off & (LN - 1)
            for b in range(parts):
                y0, y1 = (pltpu.roll(p2[q, pl.ds(at + 8 * b, 8), :], turn, 1) for q in range(2))
                v = (0.0, jnp.where(tail, y0, 0.0), jnp.where(tail, y1, y0), jnp.where(tail, 0.0, y1), 0.0)
                for q in range(4):
                    carry[b][q] = carry[b][q] + jnp.where(far, v[q], v[q + 1])
        return tuple(tuple(c) for c in carry)

    zero = jnp.zeros((8, LN), F32)
    carry = lax.fori_loop(0, (listed + UN - 1) // UN, some, ((zero,) * 4,) * parts)
    for q in range(4):
        cols = slice(q * LN, (q + 1) * LN)
        scale = 1.0 / (jnp.concatenate([carry[b][q] for b in range(parts)], 0) + REG)
        for k in range(2):
            a = k * SR
            out_ref[a : a + SR, cols] = ((own_ref[a : a + SR, cols] + up_ref[a : a + SR, cols].astype(F32)) * scale).astype(BF)


def own_step(pos, probe, own, up):
    return pl.pallas_call(
        own_kernel,
        out_shape=jax.ShapeDtypeStruct((2 * SR, OW), BF),
        in_specs=[smem(), vmem(), vmem(), vmem()],
        out_specs=vmem(),
        scratch_shapes=[pltpu.VMEM((2, PS + 2 * SR, LN), F32), pltpu.SMEM((2, 2 * NS * CAP + UN), jnp.int32)],
        compiler_params=params(8),
        name="own_step",
    )(pos, probe, own, up)


def spread_kernel(last, *refs):
    *deltas, p0_ref, p1_ref, p2_ref, p3_ref, out_ref = refs
    p = [ref[...].astype(F32) for ref in (p0_ref, p1_ref, p2_ref, p3_ref)]
    probe = (p[0] + p[1]) + (p[2] + p[3])
    w = probe[32:] + REG
    parts = [delta[...] for delta in deltas]
    if last:
        root = jnp.sqrt(w)
        parts += [probe[:16] / root, probe[16:32] / root, root]
    else:
        parts += [probe[:16] / w, probe[16:32] / w]
    at = 0
    for part in parts:
        n = part.shape[0]
        for s in range(NS):
            out_ref[s, at : at + n, :] = part.astype(BF)
        at += n


def spread(last, *args):
    rows = 2 * SR + 48 if last else 4 * SR + 32
    return pl.pallas_call(
        functools.partial(spread_kernel, last),
        out_shape=jax.ShapeDtypeStruct((NS, rows, OW), BF),
        in_specs=[vmem()] * len(args),
        out_specs=vmem(),
        compiler_params=params(8),
        name="spread",
    )(*args)


def final_kernel(obj_ref, probe_ref, recv_ref, obj_out, probe_out, grad_out):
    for s in range(NS):
        a = s * SR
        root = recv_ref[s, 2 * SR + 32 : 2 * SR + 48, :].astype(F32)
        for k in range(2):
            obj_out[k, a : a + SR, :] = obj_ref[k, a : a + SR, :] + recv_ref[s, k * SR : (k + 1) * SR, :].astype(F32)
            grad = recv_ref[s, 2 * SR + 16 * k : 2 * SR + 16 * (k + 1), :].astype(F32)
            d = grad / root
            for q in range(2):
                b = a + 16 * q
                grad_out[k, b : b + 16, :] = grad[:, q * PS : (q + 1) * PS]
                probe_out[k, b : b + 16, :] = probe_ref[k, b : b + 16, :] + d[:, q * PS : (q + 1) * PS]


def final(obj, probe, recv):
    return pl.pallas_call(
        final_kernel,
        out_shape=[
            jax.ShapeDtypeStruct((2, TH, OW), F32),
            jax.ShapeDtypeStruct((2, PS, PS), F32),
            jax.ShapeDtypeStruct((2, PS, PS), F32),
        ],
        in_specs=[vmem()] * 3,
        out_specs=[vmem()] * 3,
        compiler_params=params(8),
        name="final",
    )(obj, probe, recv)


def shifted(block, distance):
    return lax.ppermute(block, "tile", [(i, (i + distance) % NT) for i in range(NT)])


def swapped(block, bits):
    return lax.ppermute(block, "tile", [(i, i ^ bits) for i in range(NT)])


def two(x, swap):
    return (x.astype(F32) + swap.astype(F32)).astype(BF)


def four(x, swaps):
    y = [swap.astype(F32) for swap in swaps]
    return ((x.astype(F32) + y[0]) + (y[1] + y[2])).astype(BF)


def exchange(blocks):
    return lax.all_to_all(blocks, "scan", 0, 0, tiled=True)


def on_device(object_field, probe, amplitudes, positions, counts):
    pos = positions[0, 0].T
    cnt = counts[0, 0].reshape(1)
    amps, *tabs = prepare(amplitudes[0, 0])
    halo = shifted(object_field.astype(BF), -1)
    live = lax.broadcasted_iota(jnp.int32, (CAP,), 0) < cnt
    row = jnp.concatenate([jnp.where(live, pos[0] - lax.axis_index("tile") * TH + 1, 0), pos[1], cnt])
    mine = lax.broadcasted_iota(jnp.int32, (16, 1), 0) == lax.axis_index("scan")
    posblk = jnp.where(mine, row[None, :], 0).astype(BF)
    posblk = jnp.pad(posblk, ((0, 0), (0, OW - row.shape[0])))
    coded = 2 * GROUP + 1
    (send,) = patterns(pos, cnt, object_field, halo, probe, amps, tabs, posblk=posblk)
    own, part, up, tile_pos = sums(False, exchange(send))
    core = swapped(part, 1)
    up = shifted(up, 1)
    part = two(part, core)
    swaps = [swapped(part, d) for d in (2, 16, 18)]
    around = jnp.concatenate([up[2 * SR :, :coded][:NS].astype(F32), tile_pos[:NS, :coded]], 0).astype(jnp.int32)
    delta = own_step(around, probe, own, up)
    part, delta = lax.optimization_barrier((four(part, swaps), delta))
    swaps = [swapped(part, d) for d in (4, 8, 12)]
    recv = exchange(spread(False, delta, shifted(delta, -1), part, *swaps))
    send, object_field, probe = patterns(pos, cnt, object_field, halo, probe, amps, tabs, recv=recv)
    own, part, up = sums(True, exchange(send))
    core = swapped(part, 1)
    up = shifted(up, 1)
    part = two(part, core)
    swaps = [swapped(part, d) for d in (2, 16, 18)]
    delta = own_step(around, probe, own, up)
    part, delta = lax.optimization_barrier((four(part, swaps), delta))
    swaps = [swapped(part, d) for d in (4, 8, 12)]
    recv = exchange(spread(True, delta, part, *swaps))
    return tuple(final(object_field, probe, recv))


def solution(mesh):
    in_specs = (
        P(None, "tile", None),
        P(),
        P("scan", "tile", None, None, None),
        P("scan", "tile", None, None),
        P("scan", "tile"),
    )
    out_specs = (P(None, "tile", None), P(), P())
    return jax.shard_map(on_device, mesh=mesh, in_specs=in_specs, out_specs=out_specs, check_vma=False)
```

profile of v0, /device:TPU:8, one launch (start us, length us, event | category | flops | bytes accessed | tf_op | source)
XLA Modules:
  0.0 166.2 jit_solution(1734386523822894194)
XLA Ops:
  0.7 1.4 convert_element_type.62
  2.1 5.3 %collective-permute-start = (bf16[2,256,512]{2,1,0:T(8,128)(2,1)S(1)}, bf16[2,256,512]{2,1,0:T(8,128)(2,1)S(1)}, u32[]{:S(2)}, u32[]{:S(2)}) collective-permute-start(bf16[2,256,512]{2,1,0:T(8,128)(2,1)S(1)} %convert_element_type.62), channel_id=1, source_target_pairs={{0,31},{1,0},{2,1},{3,2},{4,3},{5,4},{6,5},{7,6},{8,7},{9,8},{10,9... | collective-permute-start | bytes 1572872 | tf_op jit(solution)/shard_map/ppermute | solution.py:398
  8.2 1.4 copy-done.2
  9.6 0.9 copy-done.3
  10.5 0.9 copy-done.4
  11.4 2.2 %prepare.1 = (bf16[12,256,256]{2,1,0:T(8,128)(2,1)S(1)}, bf16[512,512]{1,0:T(8,128)(2,1)S(1)}, bf16[512,512]{1,0:T(8,128)(2,1)S(1)}) custom-call(bf16[256,256]{1,0:T(8,128)(2,1)S(1)} %copy-done.4, bf16[256,256]{1,0:T(8,128)(2,1)S(1)} %copy-done.3, bf16[12,256,256]{2,1,0:T(8,128)(2,1)S(1)} %bitcast.14), custom_call_target="tpu_custom_call" | custom-call | bytes 8388608 | tf_op jit(solution)/shard_map/prepare/pallas_call | solution.py:65
  14.0 3.9 %patterns.2 = bf16[8,192,512]{2,1,0:T(8,128)(2,1)S(1)} custom-call(s32[2,12]{1,0:T(2,128)S(1)} %bitcast.17, s32[1]{0:T(128)} %bitcast.11.cnt_ref, f32[2,256,512]{2,1,0:T(8,128)S(1)} %copy-done, bf16[2,256,512]{2,1,0:T(8,128)(2,1)S(1)} %collective-permute-done.halo_ref, f32[2,256,256]{2,1,0:T(8,128)S(1)} %copy-done.1, ...), custom_call_target="tpu_custom_call" | custom-call | tf_op jit(solution)/shard_map/patterns/pallas_call | solution.py:222
  18.0 25.5 %all_to_all.20.recv_ref = bf16[8,192,512]{2,1,0:T(8,128)(2,1)S(1)} all-to-all(bf16[8,192,512]{2,1,0:T(8,128)(2,1)S(1)} %patterns.2), channel_id=1, replica_groups=mesh['scan'=8,'tile'=32] {'scan'}, dimensions={0} | all-to-all | bytes 3145728 | tf_op jit(solution)/shard_map/all_to_all | solution.py:415
  44.3 0.7 collective-permute-done.1
  45.0 1.3 collective-permute-start.4
  46.3 7.9 %collective-permute-start.3 = (bf16[48,512]{1,0:T(8,128)(2,1)S(1)}, bf16[48,512]{1,0:T(8,128)(2,1)S(1)}, u32[]{:S(2)}, u32[]{:S(2)}) collective-permute-start(bf16[48,512]{1,0:T(8,128)(2,1)S(1)} %add_convert_fusion.3), channel_id=1, source_target_pairs={{0,16},{1,17},{2,18},{3,19},{4,20},{5,21},{6,22},{7,23},{8,24},{9,... | collective-permute-start | bytes 147464 | tf_op jit(solution)/shard_map/ppermute | solution.py:402
  54.3 2.0 %own_step.2.refs_0_ = bf16[64,512]{1,0:T(8,128)(2,1)S(1)} custom-call(s32[16,25]{1,0:T(8,128)S(1)} %maximum_convert_fusion.pos_ref, f32[2,256,256]{2,1,0:T(8,128)S(1)} %copy-done.1, f32[64,512]{1,0:T(8,128)S(1)} %get-tuple-element.26.own_ref, bf16[80,512]{1,0:T(8,128)(2,1)S(1)} %collective-permute-done.5.up_ref), custom_call_target="tpu_custom_call" | custom-call | tf_op jit(solution)/shard_map/own_step/pallas_call | solution.py:326
  56.6 1.8 %collective-permute-done.2 = bf16[48,512]{1,0:T(8,128)(2,1)S(1)} collective-permute-done((bf16[48,512]{1,0:T(8,128)(2,1)S(1)}, bf16[48,512]{1,0:T(8,128)(2,1)S(1)}, u32[]{:S(2)}, u32[]{:S(2)}) %collective-permute-start.2) | collective-permute-done | bytes 49184 | tf_op jit(solution)/shard_map/ppermute | solution.py:402
  58.4 2.6 %collective-permute-start.6 = (bf16[64,512]{1,0:T(8,128)(2,1)S(1)}, bf16[64,512]{1,0:T(8,128)(2,1)S(1)}, u32[]{:S(2)}, u32[]{:S(2)}) collective-permute-start(bf16[64,512]{1,0:T(8,128)(2,1)S(1)} %own_step.2.refs_0_), channel_id=1, source_target_pairs={{0,31},{1,0},{2,1},{3,2},{4,3},{5,4},{6,5},{7,6},{8,7},{9,8},{10,9... | collective-permute-start | bytes 196616 | tf_op jit(solution)/shard_map/ppermute | solution.py:398
  61.0 1.6 collective-permute-start.9
  62.6 1.4 collective-permute-start.8
  64.0 3.5 %collective-permute-start.7 = (bf16[48,512]{1,0:T(8,128)(2,1)S(1)}, bf16[48,512]{1,0:T(8,128)(2,1)S(1)}, u32[]{:S(2)}, u32[]{:S(2)}) collective-permute-start(bf16[48,512]{1,0:T(8,128)(2,1)S(1)} %add_convert_fusion.2.refs_2_), channel_id=1, source_target_pairs={{0,4},{1,5},{2,6},{3,7},{4,0},{5,1},{6,2},{7,3},{8,12},{9,13},{10,... | collective-permute-start | bytes 147464 | tf_op jit(solution)/shard_map/ppermute | solution.py:402
  67.5 3.6 %collective-permute-done.8.refs_4_ = bf16[48,512]{1,0:T(8,128)(2,1)S(1)} collective-permute-done((bf16[48,512]{1,0:T(8,128)(2,1)S(1)}, bf16[48,512]{1,0:T(8,128)(2,1)S(1)}, u32[]{:S(2)}, u32[]{:S(2)}) %collective-permute-start.8) | collective-permute-done | bytes 49184 | tf_op jit(solution)/shard_map/ppermute | solution.py:402
  71.2 22.0 %all_to_all.21.extra_ref = bf16[8,160,512]{2,1,0:T(8,128)(2,1)S(1)} all-to-all(bf16[8,160,512]{2,1,0:T(8,128)(2,1)S(1)} %spread.2), channel_id=1, replica_groups=mesh['scan'=8,'tile'=32] {'scan'}, dimensions={0} | all-to-all | bytes 2621440 | tf_op jit(solution)/shard_map/all_to_all | solution.py:415
  93.3 4.3 %patterns.3 = (bf16[8,176,512]{2,1,0:T(8,128)(2,1)S(1)}, f32[2,256,512]{2,1,0:T(8,128)S(1)}, f32[2,256,256]{2,1,0:T(8,128)S(1)}) custom-call(s32[2,12]{1,0:T(2,128)S(1)} %bitcast.18, s32[1]{0:T(128)} %bitcast.12.cnt_ref, f32[2,256,512]{2,1,0:T(8,128)S(1)} %copy-done, bf16[2,256,512]{2,1,0:T(8,128)(2,1)S(1)} %collective-permute-done.halo_ref, ...), custom_call_target="tpu_custom_call" | custom-call | tf_op jit(solution)/shard_map/patterns/pallas_call | solution.py:222
  97.5 22.4 %all_to_all.22.recv_ref = bf16[8,176,512]{2,1,0:T(8,128)(2,1)S(1)} all-to-all(bf16[8,176,512]{2,1,0:T(8,128)(2,1)S(1)} %get-tuple-element.31), channel_id=1, replica_groups=mesh['scan'=8,'tile'=32] {'scan'}, dimensions={0} | all-to-all | bytes 2883584 | tf_op jit(solution)/shard_map/all_to_all | solution.py:415
  120.2 0.5 collective-permute-start.14
  120.7 0.7 collective-permute-done.10
  121.5 3.7 %collective-permute-start.13 = (bf16[48,512]{1,0:T(8,128)(2,1)S(1)}, bf16[48,512]{1,0:T(8,128)(2,1)S(1)}, u32[]{:S(2)}, u32[]{:S(2)}) collective-permute-start(bf16[48,512]{1,0:T(8,128)(2,1)S(1)} %add_convert_fusion.1), channel_id=1, source_target_pairs={{0,18},{1,19},{2,16},{3,17},{4,22},{5,23},{6,20},{7,21},{8,26},{9,... | collective-permute-start | bytes 147464 | tf_op jit(solution)/shard_map/ppermute | solution.py:402
  125.1 5.5 %collective-permute-start.12 = (bf16[48,512]{1,0:T(8,128)(2,1)S(1)}, bf16[48,512]{1,0:T(8,128)(2,1)S(1)}, u32[]{:S(2)}, u32[]{:S(2)}) collective-permute-start(bf16[48,512]{1,0:T(8,128)(2,1)S(1)} %add_convert_fusion.1), channel_id=1, source_target_pairs={{0,16},{1,17},{2,18},{3,19},{4,20},{5,21},{6,22},{7,23},{8,24},{9,... | collective-permute-start | bytes 147464 | tf_op jit(solution)/shard_map/ppermute | solution.py:402
  130.6 2.0 %own_step.3.refs_0_ = bf16[64,512]{1,0:T(8,128)(2,1)S(1)} custom-call(s32[16,25]{1,0:T(8,128)S(1)} %maximum_convert_fusion.pos_ref, f32[2,256,256]{2,1,0:T(8,128)S(1)} %get-tuple-element.30.probe_ref, f32[64,512]{1,0:T(8,128)S(1)} %get-tuple-element.33.own_ref, bf16[64,512]{1,0:T(8,128)(2,1)S(1)} %collective-permute-done.14.up_ref), custom_call_target="tpu_custom_call" | custom-call | tf_op jit(solution)/shard_map/own_step/pallas_call | solution.py:326
  132.9 1.8 %collective-permute-done.11 = bf16[48,512]{1,0:T(8,128)(2,1)S(1)} collective-permute-done((bf16[48,512]{1,0:T(8,128)(2,1)S(1)}, bf16[48,512]{1,0:T(8,128)(2,1)S(1)}, u32[]{:S(2)}, u32[]{:S(2)}) %collective-permute-start.11) | collective-permute-done | bytes 49184 | tf_op jit(solution)/shard_map/ppermute | solution.py:402
  134.8 5.6 %collective-permute-start.17 = (bf16[48,512]{1,0:T(8,128)(2,1)S(1)}, bf16[48,512]{1,0:T(8,128)(2,1)S(1)}, u32[]{:S(2)}, u32[]{:S(2)}) collective-permute-start(bf16[48,512]{1,0:T(8,128)(2,1)S(1)} %add_convert_fusion.refs_1_), channel_id=1, source_target_pairs={{0,12},{1,13},{2,14},{3,15},{4,8},{5,9},{6,10},{7,11},{8,4},{9,5},... | collective-permute-start | bytes 147464 | tf_op jit(solution)/shard_map/ppermute | solution.py:402
  140.3 2.5 %collective-permute-start.15 = (bf16[48,512]{1,0:T(8,128)(2,1)S(1)}, bf16[48,512]{1,0:T(8,128)(2,1)S(1)}, u32[]{:S(2)}, u32[]{:S(2)}) collective-permute-start(bf16[48,512]{1,0:T(8,128)(2,1)S(1)} %add_convert_fusion.refs_1_), channel_id=1, source_target_pairs={{0,4},{1,5},{2,6},{3,7},{4,0},{5,1},{6,2},{7,3},{8,12},{9,13},{10,... | collective-permute-start | bytes 147464 | tf_op jit(solution)/shard_map/ppermute | solution.py:402
  142.8 5.6 %collective-permute-done.16.refs_3_ = bf16[48,512]{1,0:T(8,128)(2,1)S(1)} collective-permute-done((bf16[48,512]{1,0:T(8,128)(2,1)S(1)}, bf16[48,512]{1,0:T(8,128)(2,1)S(1)}, u32[]{:S(2)}, u32[]{:S(2)}) %collective-permute-start.16) | collective-permute-done | bytes 49184 | tf_op jit(solution)/shard_map/ppermute | solution.py:402
  148.5 16.3 %all_to_all.23.recv_ref = bf16[8,112,512]{2,1,0:T(8,128)(2,1)S(1)} all-to-all(bf16[8,112,512]{2,1,0:T(8,128)(2,1)S(1)} %spread.3), channel_id=1, replica_groups=mesh['scan'=8,'tile'=32] {'scan'}, dimensions={0} | all-to-all | bytes 1835008 | tf_op jit(solution)/shard_map/all_to_all | solution.py:415
  164.8 1.4 final.1
  (44 shorter events, 2.5 us)
Async XLA Ops:
  0.6 13.4 %copy-start = (f32[2,256,512]{2,1,0:T(8,128)S(1)}, f32[2,256,512]{2,1,0:T(8,128)}, u32[]{:S(2)}) copy-start(f32[2,256,512]{2,1,0:T(8,128)} %obj_ref.3) | copy-start | bytes 3145732
  0.6 7.4 %copy-start.5 = (s32[1,1,12,2]{2,3,1,0:T(2,128)S(1)}, s32[1,1,12,2]{2,3,1,0:T(2,128)}, u32[]{:S(2)}) copy-start(s32[1,1,12,2]{2,3,1,0:T(2,128)} %param.10) | copy-start | bytes 292
  0.7 13.4 %copy-start.1 = (f32[2,256,256]{2,1,0:T(8,128)S(1)}, f32[2,256,256]{2,1,0:T(8,128)}, u32[]{:S(2)}) copy-start(f32[2,256,256]{2,1,0:T(8,128)} %probe_ref.5) | copy-start | bytes 1572868
  2.1 12.0 %collective-permute-start = (bf16[2,256,512]{2,1,0:T(8,128)(2,1)S(1)}, bf16[2,256,512]{2,1,0:T(8,128)(2,1)S(1)}, u32[]{:S(2)}, u32[]{:S(2)}) collective-permute-start(bf16[2,256,512]{2,1,0:T(8,128)(2,1)S(1)} %convert_element_type.62), channel_id=1, source_target_pairs={{0,31},{1,0},{2,1},{3,2},{4,3},{5,4},{6,5},{7,6},{8,7},{9,8},{10,9... | collective-permute-start | bytes 1572872 | tf_op jit(solution)/shard_map/ppermute | solution.py:398
  8.2 1.4 copy-start.2
  9.6 0.9 copy-start.3
  10.5 0.9 copy-start.4
  43.7 1.3 collective-permute-start.1
  43.8 10.5 %collective-permute-start.5 = (bf16[80,512]{1,0:T(8,128)(2,1)S(1)}, bf16[80,512]{1,0:T(8,128)(2,1)S(1)}, u32[]{:S(2)}, u32[]{:S(2)}) collective-permute-start(bf16[80,512]{1,0:T(8,128)(2,1)S(1)} %get-tuple-element.24), channel_id=1, source_target_pairs={{0,1},{1,2},{2,3},{3,4},{4,5},{5,6},{6,7},{7,8},{8,9},{9,10},{10,1... | collective-permute-start | bytes 245768 | tf_op jit(solution)/shard_map/ppermute | solution.py:398
  45.0 11.3 %collective-permute-start.4 = (bf16[48,512]{1,0:T(8,128)(2,1)S(1)}, bf16[48,512]{1,0:T(8,128)(2,1)S(1)}, u32[]{:S(2)}, u32[]{:S(2)}) collective-permute-start(bf16[48,512]{1,0:T(8,128)(2,1)S(1)} %add_convert_fusion.3), channel_id=1, source_target_pairs={{0,18},{1,19},{2,16},{3,17},{4,22},{5,23},{6,20},{7,21},{8,26},{9,... | collective-permute-start | bytes 147464 | tf_op jit(solution)/shard_map/ppermute | solution.py:402
  46.3 10.2 %collective-permute-start.3 = (bf16[48,512]{1,0:T(8,128)(2,1)S(1)}, bf16[48,512]{1,0:T(8,128)(2,1)S(1)}, u32[]{:S(2)}, u32[]{:S(2)}) collective-permute-start(bf16[48,512]{1,0:T(8,128)(2,1)S(1)} %add_convert_fusion.3), channel_id=1, source_target_pairs={{0,16},{1,17},{2,18},{3,19},{4,20},{5,21},{6,22},{7,23},{8,24},{9,... | collective-permute-start | bytes 147464 | tf_op jit(solution)/shard_map/ppermute | solution.py:402
  54.2 4.1 %collective-permute-start.2 = (bf16[48,512]{1,0:T(8,128)(2,1)S(1)}, bf16[48,512]{1,0:T(8,128)(2,1)S(1)}, u32[]{:S(2)}, u32[]{:S(2)}) collective-permute-start(bf16[48,512]{1,0:T(8,128)(2,1)S(1)} %add_convert_fusion.3), channel_id=1, source_target_pairs={{0,2},{1,3},{2,0},{3,1},{4,6},{5,7},{6,4},{7,5},{8,10},{9,11},{10,... | collective-permute-start | bytes 147464 | tf_op jit(solution)/shard_map/ppermute | solution.py:402
  58.4 12.7 %collective-permute-start.6 = (bf16[64,512]{1,0:T(8,128)(2,1)S(1)}, bf16[64,512]{1,0:T(8,128)(2,1)S(1)}, u32[]{:S(2)}, u32[]{:S(2)}) collective-permute-start(bf16[64,512]{1,0:T(8,128)(2,1)S(1)} %own_step.2.refs_0_), channel_id=1, source_target_pairs={{0,31},{1,0},{2,1},{3,2},{4,3},{5,4},{6,5},{7,6},{8,7},{9,8},{10,9... | collective-permute-start | bytes 196616 | tf_op jit(solution)/shard_map/ppermute | solution.py:398
  61.0 6.5 %collective-permute-start.9 = (bf16[48,512]{1,0:T(8,128)(2,1)S(1)}, bf16[48,512]{1,0:T(8,128)(2,1)S(1)}, u32[]{:S(2)}, u32[]{:S(2)}) collective-permute-start(bf16[48,512]{1,0:T(8,128)(2,1)S(1)} %add_convert_fusion.2.refs_2_), channel_id=1, source_target_pairs={{0,12},{1,13},{2,14},{3,15},{4,8},{5,9},{6,10},{7,11},{8,4},{9,5},... | collective-permute-start | bytes 147464 | tf_op jit(solution)/shard_map/ppermute | solution.py:402
  62.6 8.5 %collective-permute-start.8 = (bf16[48,512]{1,0:T(8,128)(2,1)S(1)}, bf16[48,512]{1,0:T(8,128)(2,1)S(1)}, u32[]{:S(2)}, u32[]{:S(2)}) collective-permute-start(bf16[48,512]{1,0:T(8,128)(2,1)S(1)} %add_convert_fusion.2.refs_2_), channel_id=1, source_target_pairs={{0,8},{1,9},{2,10},{3,11},{4,12},{5,13},{6,14},{7,15},{8,0},{9,1},... | collective-permute-start | bytes 147464 | tf_op jit(solution)/shard_map/ppermute | solution.py:402
  64.0 7.1 %collective-permute-start.7 = (bf16[48,512]{1,0:T(8,128)(2,1)S(1)}, bf16[48,512]{1,0:T(8,128)(2,1)S(1)}, u32[]{:S(2)}, u32[]{:S(2)}) collective-permute-start(bf16[48,512]{1,0:T(8,128)(2,1)S(1)} %add_convert_fusion.2.refs_2_), channel_id=1, source_target_pairs={{0,4},{1,5},{2,6},{3,7},{4,0},{5,1},{6,2},{7,3},{8,12},{9,13},{10,... | collective-permute-start | bytes 147464 | tf_op jit(solution)/shard_map/ppermute | solution.py:402
  120.1 1.3 collective-permute-start.10
  120.2 10.4 %collective-permute-start.14 = (bf16[64,512]{1,0:T(8,128)(2,1)S(1)}, bf16[64,512]{1,0:T(8,128)(2,1)S(1)}, u32[]{:S(2)}, u32[]{:S(2)}) collective-permute-start(bf16[64,512]{1,0:T(8,128)(2,1)S(1)} %get-tuple-element.34), channel_id=1, source_target_pairs={{0,1},{1,2},{2,3},{3,4},{4,5},{5,6},{6,7},{7,8},{8,9},{9,10},{10,1... | collective-permute-start | bytes 196616 | tf_op jit(solution)/shard_map/ppermute | solution.py:398
  121.5 11.2 %collective-permute-start.13 = (bf16[48,512]{1,0:T(8,128)(2,1)S(1)}, bf16[48,512]{1,0:T(8,128)(2,1)S(1)}, u32[]{:S(2)}, u32[]{:S(2)}) collective-permute-start(bf16[48,512]{1,0:T(8,128)(2,1)S(1)} %add_convert_fusion.1), channel_id=1, source_target_pairs={{0,18},{1,19},{2,16},{3,17},{4,22},{5,23},{6,20},{7,21},{8,26},{9,... | collective-permute-start | bytes 147464 | tf_op jit(solution)/shard_map/ppermute | solution.py:402
  125.1 7.8 %collective-permute-start.12 = (bf16[48,512]{1,0:T(8,128)(2,1)S(1)}, bf16[48,512]{1,0:T(8,128)(2,1)S(1)}, u32[]{:S(2)}, u32[]{:S(2)}) collective-permute-start(bf16[48,512]{1,0:T(8,128)(2,1)S(1)} %add_convert_fusion.1), channel_id=1, source_target_pairs={{0,16},{1,17},{2,18},{3,19},{4,20},{5,21},{6,22},{7,23},{8,24},{9,... | collective-permute-start | bytes 147464 | tf_op jit(solution)/shard_map/ppermute | solution.py:402
  130.6 4.1 %collective-permute-start.11 = (bf16[48,512]{1,0:T(8,128)(2,1)S(1)}, bf16[48,512]{1,0:T(8,128)(2,1)S(1)}, u32[]{:S(2)}, u32[]{:S(2)}) collective-permute-start(bf16[48,512]{1,0:T(8,128)(2,1)S(1)} %add_convert_fusion.1), channel_id=1, source_target_pairs={{0,2},{1,3},{2,0},{3,1},{4,6},{5,7},{6,4},{7,5},{8,10},{9,11},{10,... | collective-permute-start | bytes 147464 | tf_op jit(solution)/shard_map/ppermute | solution.py:402
  134.8 8.0 %collective-permute-start.17 = (bf16[48,512]{1,0:T(8,128)(2,1)S(1)}, bf16[48,512]{1,0:T(8,128)(2,1)S(1)}, u32[]{:S(2)}, u32[]{:S(2)}) collective-permute-start(bf16[48,512]{1,0:T(8,128)(2,1)S(1)} %add_convert_fusion.refs_1_), channel_id=1, source_target_pairs={{0,12},{1,13},{2,14},{3,15},{4,8},{5,9},{6,10},{7,11},{8,4},{9,5},... | collective-permute-start | bytes 147464 | tf_op jit(solution)/shard_map/ppermute | solution.py:402
  140.3 8.1 %collective-permute-start.16 = (bf16[48,512]{1,0:T(8,128)(2,1)S(1)}, bf16[48,512]{1,0:T(8,128)(2,1)S(1)}, u32[]{:S(2)}, u32[]{:S(2)}) collective-permute-start(bf16[48,512]{1,0:T(8,128)(2,1)S(1)} %add_convert_fusion.refs_1_), channel_id=1, source_target_pairs={{0,8},{1,9},{2,10},{3,11},{4,12},{5,13},{6,14},{7,15},{8,0},{9,1},... | collective-permute-start | bytes 147464 | tf_op jit(solution)/shard_map/ppermute | solution.py:402
  140.3 8.1 %collective-permute-start.15 = (bf16[48,512]{1,0:T(8,128)(2,1)S(1)}, bf16[48,512]{1,0:T(8,128)(2,1)S(1)}, u32[]{:S(2)}, u32[]{:S(2)}) collective-permute-start(bf16[48,512]{1,0:T(8,128)(2,1)S(1)} %add_convert_fusion.refs_1_), channel_id=1, source_target_pairs={{0,4},{1,5},{2,6},{3,7},{4,0},{5,1},{6,2},{7,3},{8,12},{9,13},{10,... | collective-permute-start | bytes 147464 | tf_op jit(solution)/shard_map/ppermute | solution.py:402
where the time goes:
time: 166 us
  blocking collectives  86.3 us (52%)
  starting transfers between devices  42 us (25%)
  Pallas kernels  16.4 us (10%)
  waiting for transfers between devices  15.2 us (9%)
  local copies, waits for them, and re-layouts  3.24 us (2%)
  other arithmetic  1.67 us (1%)
    all_to_all x4, blocking collectives, exchange(): return lax.all_to_all(blocks, 'scan', 0, 0, tiled=True)  86.3 us
    ppermute x14, starting transfers between devices, swapped(): return lax.ppermute(block, 'tile', [(i, i ^ bits) for i in range(NT)])  33.1 us
    ppermute x14, waiting for transfers between devices, swapped(): return lax.ppermute(block, 'tile', [(i, i ^ bits) for i in range(NT)])  14.8 us
    ppermute x4, starting transfers between devices, shifted(): lax.ppermute(block, 'tile', [(i, (i + distance) % NT) for i in range(NT)])  8.85 us
    pallas_call x2, Pallas kernels, patterns(): pl.pallas_call(functools.partial(pattern_kernel, first), out_shape=out, i...  8.19 us
    pallas_call x2, Pallas kernels, own_step(): pl.pallas_call(own_kernel, out_shape=jax.ShapeDtypeStruct((2 * SR, OW), B...  4.03 us
  transfers between devices with their start and end apart: 18, of which 9 were waited for; matrix products, arithmetic and copies ran while one was open for 0% of the time, Pallas kernels for 4%

commit v1 on v0

--- a/solution.py
+++ b/solution.py
@@ -41,37 +41,28 @@
     return c, s
 
 
-def table_arrays():
-    return [jnp.asarray(t.astype(jnp.bfloat16)) for t in tables()]
-
-
-def prepare_kernel(c_ref, s_ref, amp_ref, amp_out, m1_ref, m2_ref, sems):
-    copies = [pltpu.make_async_copy(amp_ref.at[j], amp_out.at[j], sems.at[j]) for j in range(CAP)]
-    for copy in copies:
-        copy.start()
-    c = c_ref[...]
+def prepare_kernel(c_ref, s_ref, amp_ref, m1_ref, m2_ref):
+    c = c_ref[...].astype(BF)
     s = s_ref[...]
-    for table, upper, lower in ((m1_ref, -s, s), (m2_ref, s, -s)):
+    for table, sign in ((m1_ref, -1.0), (m2_ref, 1.0)):
         table[:PS, :PS] = c
-        table[:PS, PS:] = upper
-        table[PS:, :PS] = lower
+        table[:PS, PS:] = (sign * s).astype(BF)
+        table[PS:, :PS] = (-sign * s).astype(BF)
         table[PS:, PS:] = c
-    for copy in copies:
-        copy.wait()
 
 
 def prepare(amps):
     table = jax.ShapeDtypeStruct((2 * PS, 2 * PS), BF)
+    rounded = [jnp.asarray(t.astype(jnp.bfloat16).astype(np.float32)) for t in tables()]
     return pl.pallas_call(
         prepare_kernel,
-        out_shape=[jax.ShapeDtypeStruct(amps.shape, BF), table, table],
-        in_specs=[vmem(), vmem(), pl.BlockSpec(memory_space=pltpu.HBM)],
-        out_specs=[vmem()] * 3,
-        scratch_shapes=[pltpu.SemaphoreType.DMA((CAP,))],
+        out_shape=[table, table],
+        in_specs=[vmem()] * 3,
+        out_specs=[vmem()] * 2,
         compiler_params=params(8),
         cost_estimate=pl.CostEstimate(flops=0, bytes_accessed=8 << 20, transcendentals=0),
         name="prepare",
-    )(*table_arrays(), amps)
+    )(*rounded, amps)
 
 
 def pattern_kernel(first, pos_ref, cnt_ref, obj_ref, halo_ref, probe_ref, amp_ref, extra_ref, m1, m2, *rest):
@@ -418,7 +409,8 @@
 def on_device(object_field, probe, amplitudes, positions, counts):
     pos = positions[0, 0].T
     cnt = counts[0, 0].reshape(1)
-    amps, *tabs = prepare(amplitudes[0, 0])
+    amps = amplitudes[0, 0]
+    tabs = prepare(amps)
     halo = shifted(object_field.astype(BF), -1)
     live = lax.broadcasted_iota(jnp.int32, (CAP,), 0) < cnt
     row = jnp.concatenate([jnp.where(live, pos[0] - lax.axis_index("tile") * TH + 1, 0), pos[1], cnt])
@@ -444,7 +436,7 @@
     part = two(part, core)
     swaps = [swapped(part, d) for d in (2, 16, 18)]
     delta = own_step(around, probe, own, up)
-    part, delta = lax.optimization_barrier((four(part, swaps), delta))
+    part = four(part, swaps)
     swaps = [swapped(part, d) for d in (4, 8, 12)]
     recv = exchange(spread(True, delta, part, *swaps))
     return tuple(final(object_field, probe, recv))

time: 166 us -> 166 us (level)
  starting transfers between devices: 42 us -> 30.6 us
  Pallas kernels: 16.4 us -> 27.7 us
  blocking collectives: 86.3 us -> 82.2 us
  waiting for transfers between devices: 15.2 us -> 17.4 us
    pallas_call x2, Pallas kernels: 8.19 us -> 20.4 us  [patterns(): pl.pallas_call(functools.partial(pattern_kernel, first), out_shape=out, i...]
    ppermute x14, starting transfers between devices: 33.1 us -> 23 us  [swapped(): return lax.ppermute(block, 'tile', [(i, i ^ bits) for i in range(NT)])]
    ppermute x4, waiting for transfers between devices: 0.43 us -> 5.52 us  [shifted(): lax.ppermute(block, 'tile', [(i, (i + distance) % NT) for i in range(NT)])]
    all_to_all x4, blocking collectives: 86.3 us -> 82.2 us  [exchange(): return lax.all_to_all(blocks, 'scan', 0, 0, tiled=True)]
    ppermute x14, waiting for transfers between devices: 14.8 us -> 11.9 us  [swapped(): return lax.ppermute(block, 'tile', [(i, i ^ bits) for i in range(NT)])]
    pallas_call x1, Pallas kernels: 2.19 us -> 0.07 us  [prepare(): pl.pallas_call(prepare_kernel, out_shape=[table, table], in_specs=[vmem()...]
  transfers between devices with their start and end apart: 18 -> 18, of which waited for: 9 -> 9; matrix products, arithmetic and copies ran while one was open for 0% -> 1% of each run, Pallas kernels for 4% -> 3%
where the time goes in v1:
time: 166 us; the launch traced here: 165 us
  blocking collectives  82.2 us (50%)
  starting transfers between devices  30.6 us (18%)
  Pallas kernels  27.7 us (17%)
  waiting for transfers between devices  17.4 us (10%)
  other arithmetic  3.14 us (2%)
  local copies, waits for them, and re-layouts  2.61 us (2%)
    all_to_all x4, blocking collectives, exchange(): return lax.all_to_all(blocks, 'scan', 0, 0, tiled=True)  82.2 us
    ppermute x14, starting transfers between devices, swapped(): return lax.ppermute(block, 'tile', [(i, i ^ bits) for i in range(NT)])  23 us
    pallas_call x2, Pallas kernels, patterns(): pl.pallas_call(functools.partial(pattern_kernel, first), out_shape=out, i...  20.4 us
    ppermute x14, waiting for transfers between devices, swapped(): return lax.ppermute(block, 'tile', [(i, i ^ bits) for i in range(NT)])  11.9 us
    ppermute x4, starting transfers between devices, shifted(): lax.ppermute(block, 'tile', [(i, (i + distance) % NT) for i in range(NT)])  7.55 us
    ppermute x4, waiting for transfers between devices, shifted(): lax.ppermute(block, 'tile', [(i, (i + distance) % NT) for i in range(NT)])  5.52 us
    pallas_call x2, Pallas kernels, own_step(): pl.pallas_call(own_kernel, out_shape=jax.ShapeDtypeStruct((2 * SR, OW), B...  5.24 us
  transfers between devices with their start and end apart: 18, of which 9 were waited for; matrix products, arithmetic and copies ran while one was open for 1% of the time, Pallas kernels for 3%

profile of v1, /device:TPU:8, one launch (start us, length us, event | category | flops | bytes accessed | tf_op | source)
XLA Modules:
  0.0 165.1 jit_solution(16379637771306898739)
XLA Ops:
  0.6 2.2 %convert_element_type.62 = bf16[2,256,512]{2,1,0:T(8,128)(2,1)} convert(f32[2,256,512]{2,1,0:T(8,128)} %obj_ref.3) | non-fusion elementwise | flops 262144 | bytes 1572864 | tf_op jit(solution)/shard_map/convert_element_type | solution.py:414
  2.8 5.2 %collective-permute-start = (bf16[2,256,512]{2,1,0:T(8,128)(2,1)}, bf16[2,256,512]{2,1,0:T(8,128)(2,1)}, u32[]{:S(2)}, u32[]{:S(2)}) collective-permute-start(bf16[2,256,512]{2,1,0:T(8,128)(2,1)} %convert_element_type.62), channel_id=1, source_target_pairs={{0,31},{1,0},{2,1},{3,2},{4,3},{5,4},{6,5},{7,6},{8,7},{9,8},{10,9... | collective-permute-start | bytes 1572872 | tf_op jit(solution)/shard_map/ppermute | solution.py:389
  8.7 0.7 slice_bitcast_fusion
  9.4 0.7 compare_select_fusion
  10.2 0.9 copy-done.3
  11.2 0.9 copy-done.4
  12.2 2.8 %collective-permute-done.halo_ref = bf16[2,256,512]{2,1,0:T(8,128)(2,1)} collective-permute-done((bf16[2,256,512]{2,1,0:T(8,128)(2,1)}, bf16[2,256,512]{2,1,0:T(8,128)(2,1)}, u32[]{:S(2)}, u32[]{:S(2)}) %collective-permute-start) | collective-permute-done | bytes 524320 | tf_op jit(solution)/shard_map/ppermute | solution.py:389
  15.1 10.0 %patterns.2 = bf16[8,192,512]{2,1,0:T(8,128)(2,1)S(1)} custom-call(s32[2,12]{1,0:T(2,128)S(1)} %bitcast.19, s32[1]{0:T(128)} %bitcast.11.cnt_ref, f32[2,256,512]{2,1,0:T(8,128)S(1)} %copy-done.1, bf16[2,256,512]{2,1,0:T(8,128)(2,1)} %collective-permute-done.halo_ref, f32[2,256,256]{2,1,0:T(8,128)S(1)} %copy-done.2, bf16[12,256,256]{2,1,0:T(8,128)(2,1)S(1)} %bitcast.15, ...), custom_call_target="tpu_custom_call" | custom-call | tf_op jit(solution)/shard_map/patterns/pallas_call | solution.py:213
  25.1 24.4 %all_to_all.20.recv_ref = bf16[8,192,512]{2,1,0:T(8,128)(2,1)S(1)} all-to-all(bf16[8,192,512]{2,1,0:T(8,128)(2,1)S(1)} %patterns.2), channel_id=1, replica_groups=mesh['scan'=8,'tile'=32] {'scan'}, dimensions={0} | all-to-all | bytes 3145728 | tf_op jit(solution)/shard_map/all_to_all | solution.py:406
  50.3 0.7 collective-permute-done.1
  51.2 3.4 %collective-permute-start.2 = (bf16[48,512]{1,0:T(8,128)(2,1)S(1)}, bf16[48,512]{1,0:T(8,128)(2,1)S(1)}, u32[]{:S(2)}, u32[]{:S(2)}) collective-permute-start(bf16[48,512]{1,0:T(8,128)(2,1)S(1)} %add_convert_fusion.3), channel_id=1, source_target_pairs={{0,2},{1,3},{2,0},{3,1},{4,6},{5,7},{6,4},{7,5},{8,10},{9,11},{10,... | collective-permute-start | bytes 147464 | tf_op jit(solution)/shard_map/ppermute | solution.py:393
  54.6 2.7 %collective-permute-done.5.up_ref = bf16[80,512]{1,0:T(8,128)(2,1)S(1)} collective-permute-done((bf16[80,512]{1,0:T(8,128)(2,1)S(1)}, bf16[80,512]{1,0:T(8,128)(2,1)S(1)}, u32[]{:S(2)}, u32[]{:S(2)}) %collective-permute-start.5) | collective-permute-done | bytes 81952 | tf_op jit(solution)/shard_map/ppermute | solution.py:389
  57.3 2.6 %own_step.2.refs_0_ = bf16[64,512]{1,0:T(8,128)(2,1)S(1)} custom-call(s32[16,25]{1,0:T(8,128)S(1)} %maximum_convert_fusion.pos_ref, f32[2,256,256]{2,1,0:T(8,128)S(1)} %copy-done.2, f32[64,512]{1,0:T(8,128)S(1)} %get-tuple-element.22.own_ref, bf16[80,512]{1,0:T(8,128)(2,1)S(1)} %collective-permute-done.5.up_ref), custom_call_target="tpu_custom_call" | custom-call | tf_op jit(solution)/shard_map/own_step/pallas_call | solution.py:317
  60.0 1.9 %collective-permute-start.6 = (bf16[64,512]{1,0:T(8,128)(2,1)S(1)}, bf16[64,512]{1,0:T(8,128)(2,1)S(1)}, u32[]{:S(2)}, u32[]{:S(2)}) collective-permute-start(bf16[64,512]{1,0:T(8,128)(2,1)S(1)} %own_step.2.refs_0_), channel_id=1, source_target_pairs={{0,31},{1,0},{2,1},{3,2},{4,3},{5,4},{6,5},{7,6},{8,7},{9,8},{10,9... | collective-permute-start | bytes 196616 | tf_op jit(solution)/shard_map/ppermute | solution.py:389
  61.9 3.0 %collective-permute-start.9 = (bf16[48,512]{1,0:T(8,128)(2,1)S(1)}, bf16[48,512]{1,0:T(8,128)(2,1)S(1)}, u32[]{:S(2)}, u32[]{:S(2)}) collective-permute-start(bf16[48,512]{1,0:T(8,128)(2,1)S(1)} %add_convert_fusion.2.refs_2_), channel_id=1, source_target_pairs={{0,12},{1,13},{2,14},{3,15},{4,8},{5,9},{6,10},{7,11},{8,4},{9,5},... | collective-permute-start | bytes 147464 | tf_op jit(solution)/shard_map/ppermute | solution.py:393
  64.9 1.0 collective-permute-start.8
  65.9 2.5 %collective-permute-start.7 = (bf16[48,512]{1,0:T(8,128)(2,1)S(1)}, bf16[48,512]{1,0:T(8,128)(2,1)S(1)}, u32[]{:S(2)}, u32[]{:S(2)}) collective-permute-start(bf16[48,512]{1,0:T(8,128)(2,1)S(1)} %add_convert_fusion.2.refs_2_), channel_id=1, source_target_pairs={{0,4},{1,5},{2,6},{3,7},{4,0},{5,1},{6,2},{7,3},{8,12},{9,13},{10,... | collective-permute-start | bytes 147464 | tf_op jit(solution)/shard_map/ppermute | solution.py:393
  68.6 4.7 %collective-permute-done.8.refs_4_ = bf16[48,512]{1,0:T(8,128)(2,1)S(1)} collective-permute-done((bf16[48,512]{1,0:T(8,128)(2,1)S(1)}, bf16[48,512]{1,0:T(8,128)(2,1)S(1)}, u32[]{:S(2)}, u32[]{:S(2)}) %collective-permute-start.8) | collective-permute-done | bytes 49184 | tf_op jit(solution)/shard_map/ppermute | solution.py:393
  73.4 21.9 %all_to_all.21.extra_ref = bf16[8,160,512]{2,1,0:T(8,128)(2,1)S(1)} all-to-all(bf16[8,160,512]{2,1,0:T(8,128)(2,1)S(1)} %spread.2), channel_id=1, replica_groups=mesh['scan'=8,'tile'=32] {'scan'}, dimensions={0} | all-to-all | bytes 2621440 | tf_op jit(solution)/shard_map/all_to_all | solution.py:406
  95.3 10.4 %patterns.3 = (bf16[8,176,512]{2,1,0:T(8,128)(2,1)S(1)}, f32[2,256,512]{2,1,0:T(8,128)S(1)}, f32[2,256,256]{2,1,0:T(8,128)S(1)}) custom-call(s32[2,12]{1,0:T(2,128)S(1)} %bitcast.20, s32[1]{0:T(128)} %bitcast.12.cnt_ref, f32[2,256,512]{2,1,0:T(8,128)S(1)} %copy-done.1, bf16[2,256,512]{2,1,0:T(8,128)(2,1)} %collective-permute-done.halo_ref, ...), custom_call_target="tpu_custom_call" | custom-call | tf_op jit(solution)/shard_map/patterns/pallas_call | solution.py:213
  105.7 20.0 %all_to_all.22.recv_ref = bf16[8,176,512]{2,1,0:T(8,128)(2,1)S(1)} all-to-all(bf16[8,176,512]{2,1,0:T(8,128)(2,1)S(1)} %get-tuple-element.27), channel_id=1, replica_groups=mesh['scan'=8,'tile'=32] {'scan'}, dimensions={0} | all-to-all | bytes 2883584 | tf_op jit(solution)/shard_map/all_to_all | solution.py:406
  126.0 1.2 collective-permute-done.11
  127.3 1.1 collective-permute-start.13
  128.4 2.4 %collective-permute-start.12 = (bf16[48,512]{1,0:T(8,128)(2,1)S(1)}, bf16[48,512]{1,0:T(8,128)(2,1)S(1)}, u32[]{:S(2)}, u32[]{:S(2)}) collective-permute-start(bf16[48,512]{1,0:T(8,128)(2,1)S(1)} %add_convert_fusion.1), channel_id=1, source_target_pairs={{0,2},{1,3},{2,0},{3,1},{4,6},{5,7},{6,4},{7,5},{8,10},{9,11},{10,... | collective-permute-start | bytes 147464 | tf_op jit(solution)/shard_map/ppermute | solution.py:393
  130.8 1.7 %collective-permute-done.14 = bf16[48,512]{1,0:T(8,128)(2,1)S(1)} collective-permute-done((bf16[48,512]{1,0:T(8,128)(2,1)S(1)}, bf16[48,512]{1,0:T(8,128)(2,1)S(1)}, u32[]{:S(2)}, u32[]{:S(2)}) %collective-permute-start.14) | collective-permute-done | bytes 49184 | tf_op jit(solution)/shard_map/ppermute | solution.py:393
  132.9 6.8 %collective-permute-start.17 = (bf16[48,512]{1,0:T(8,128)(2,1)S(1)}, bf16[48,512]{1,0:T(8,128)(2,1)S(1)}, u32[]{:S(2)}, u32[]{:S(2)}) collective-permute-start(bf16[48,512]{1,0:T(8,128)(2,1)S(1)} %add_convert_fusion.refs_1_), channel_id=1, source_target_pairs={{0,12},{1,13},{2,14},{3,15},{4,8},{5,9},{6,10},{7,11},{8,4},{9,5},... | collective-permute-start | bytes 147464 | tf_op jit(solution)/shard_map/ppermute | solution.py:393
  139.7 0.7 collective-permute-start.16
  140.4 1.8 %collective-permute-start.15 = (bf16[48,512]{1,0:T(8,128)(2,1)S(1)}, bf16[48,512]{1,0:T(8,128)(2,1)S(1)}, u32[]{:S(2)}, u32[]{:S(2)}) collective-permute-start(bf16[48,512]{1,0:T(8,128)(2,1)S(1)} %add_convert_fusion.refs_1_), channel_id=1, source_target_pairs={{0,4},{1,5},{2,6},{3,7},{4,0},{5,1},{6,2},{7,3},{8,12},{9,13},{10,... | collective-permute-start | bytes 147464 | tf_op jit(solution)/shard_map/ppermute | solution.py:393
  142.1 2.6 %own_step.3.refs_0_ = bf16[64,512]{1,0:T(8,128)(2,1)S(1)} custom-call(s32[16,25]{1,0:T(8,128)S(1)} %maximum_convert_fusion.pos_ref, f32[2,256,256]{2,1,0:T(8,128)S(1)} %get-tuple-element.26.probe_ref, f32[64,512]{1,0:T(8,128)S(1)} %get-tuple-element.28.own_ref, bf16[64,512]{1,0:T(8,128)(2,1)S(1)} %collective-permute-done.10.up_ref), custom_call_target="tpu_custom_call" | custom-call | tf_op jit(solution)/shard_map/own_step/pallas_call | solution.py:317
  144.8 3.0 %collective-permute-done.16.refs_3_ = bf16[48,512]{1,0:T(8,128)(2,1)S(1)} collective-permute-done((bf16[48,512]{1,0:T(8,128)(2,1)S(1)}, bf16[48,512]{1,0:T(8,128)(2,1)S(1)}, u32[]{:S(2)}, u32[]{:S(2)}) %collective-permute-start.16) | collective-permute-done | bytes 49184 | tf_op jit(solution)/shard_map/ppermute | solution.py:393
  147.8 15.9 %all_to_all.23.recv_ref = bf16[8,112,512]{2,1,0:T(8,128)(2,1)S(1)} all-to-all(bf16[8,112,512]{2,1,0:T(8,128)(2,1)S(1)} %spread.3), channel_id=1, replica_groups=mesh['scan'=8,'tile'=32] {'scan'}, dimensions={0} | all-to-all | bytes 1835008 | tf_op jit(solution)/shard_map/all_to_all | solution.py:406
  163.7 1.4 final.1
  (44 shorter events, 2.4 us)
Async XLA Ops:
  0.6 9.6 %copy-start = (bf16[1,1,12,256,256]{4,3,2,1,0:T(8,128)(2,1)S(1)}, bf16[1,1,12,256,256]{4,3,2,1,0:T(8,128)(2,1)}, u32[]{:S(2)}) copy-start(bf16[1,1,12,256,256]{4,3,2,1,0:T(8,128)(2,1)} %param.9) | copy-start | bytes 4718596
  2.8 12.2 %copy-start.1 = (f32[2,256,512]{2,1,0:T(8,128)S(1)}, f32[2,256,512]{2,1,0:T(8,128)}, u32[]{:S(2)}) copy-start(f32[2,256,512]{2,1,0:T(8,128)} %obj_ref.3) | copy-start | bytes 3145732
  2.8 12.2 %copy-start.2 = (f32[2,256,256]{2,1,0:T(8,128)S(1)}, f32[2,256,256]{2,1,0:T(8,128)}, u32[]{:S(2)}) copy-start(f32[2,256,256]{2,1,0:T(8,128)} %probe_ref.5) | copy-start | bytes 1572868
  2.8 12.2 %collective-permute-start = (bf16[2,256,512]{2,1,0:T(8,128)(2,1)}, bf16[2,256,512]{2,1,0:T(8,128)(2,1)}, u32[]{:S(2)}, u32[]{:S(2)}) collective-permute-start(bf16[2,256,512]{2,1,0:T(8,128)(2,1)} %convert_element_type.62), channel_id=1, source_target_pairs={{0,31},{1,0},{2,1},{3,2},{4,3},{5,4},{6,5},{7,6},{8,7},{9,8},{10,9... | collective-permute-start | bytes 1572872 | tf_op jit(solution)/shard_map/ppermute | solution.py:389
  10.2 1.0 copy-start.3
  11.2 0.9 copy-start.4
  12.1 2.9 %copy-start.5 = (s32[1,1,12,2]{2,3,1,0:T(2,128)S(1)}, s32[1,1,12,2]{2,3,1,0:T(2,128)}, u32[]{:S(2)}) copy-start(s32[1,1,12,2]{2,3,1,0:T(2,128)} %param.10) | copy-start | bytes 292
  49.7 1.3 collective-permute-start.1
  49.8 7.5 %collective-permute-start.5 = (bf16[80,512]{1,0:T(8,128)(2,1)S(1)}, bf16[80,512]{1,0:T(8,128)(2,1)S(1)}, u32[]{:S(2)}, u32[]{:S(2)}) collective-permute-start(bf16[80,512]{1,0:T(8,128)(2,1)S(1)} %get-tuple-element.20), channel_id=1, source_target_pairs={{0,1},{1,2},{2,3},{3,4},{4,5},{5,6},{6,7},{7,8},{8,9},{9,10},{10,1... | collective-permute-start | bytes 245768 | tf_op jit(solution)/shard_map/ppermute | solution.py:389
  51.0 8.9 %collective-permute-start.4 = (bf16[48,512]{1,0:T(8,128)(2,1)S(1)}, bf16[48,512]{1,0:T(8,128)(2,1)S(1)}, u32[]{:S(2)}, u32[]{:S(2)}) collective-permute-start(bf16[48,512]{1,0:T(8,128)(2,1)S(1)} %add_convert_fusion.3), channel_id=1, source_target_pairs={{0,18},{1,19},{2,16},{3,17},{4,22},{5,23},{6,20},{7,21},{8,26},{9,... | collective-permute-start | bytes 147464 | tf_op jit(solution)/shard_map/ppermute | solution.py:393
  51.1 8.8 %collective-permute-start.3 = (bf16[48,512]{1,0:T(8,128)(2,1)S(1)}, bf16[48,512]{1,0:T(8,128)(2,1)S(1)}, u32[]{:S(2)}, u32[]{:S(2)}) collective-permute-start(bf16[48,512]{1,0:T(8,128)(2,1)S(1)} %add_convert_fusion.3), channel_id=1, source_target_pairs={{0,16},{1,17},{2,18},{3,19},{4,20},{5,21},{6,22},{7,23},{8,24},{9,... | collective-permute-start | bytes 147464 | tf_op jit(solution)/shard_map/ppermute | solution.py:393
  51.2 8.7 %collective-permute-start.2 = (bf16[48,512]{1,0:T(8,128)(2,1)S(1)}, bf16[48,512]{1,0:T(8,128)(2,1)S(1)}, u32[]{:S(2)}, u32[]{:S(2)}) collective-permute-start(bf16[48,512]{1,0:T(8,128)(2,1)S(1)} %add_convert_fusion.3), channel_id=1, source_target_pairs={{0,2},{1,3},{2,0},{3,1},{4,6},{5,7},{6,4},{7,5},{8,10},{9,11},{10,... | collective-permute-start | bytes 147464 | tf_op jit(solution)/shard_map/ppermute | solution.py:393
  60.0 13.3 %collective-permute-start.6 = (bf16[64,512]{1,0:T(8,128)(2,1)S(1)}, bf16[64,512]{1,0:T(8,128)(2,1)S(1)}, u32[]{:S(2)}, u32[]{:S(2)}) collective-permute-start(bf16[64,512]{1,0:T(8,128)(2,1)S(1)} %own_step.2.refs_0_), channel_id=1, source_target_pairs={{0,31},{1,0},{2,1},{3,2},{4,3},{5,4},{6,5},{7,6},{8,7},{9,8},{10,9... | collective-permute-start | bytes 196616 | tf_op jit(solution)/shard_map/ppermute | solution.py:389
  61.9 6.7 %collective-permute-start.9 = (bf16[48,512]{1,0:T(8,128)(2,1)S(1)}, bf16[48,512]{1,0:T(8,128)(2,1)S(1)}, u32[]{:S(2)}, u32[]{:S(2)}) collective-permute-start(bf16[48,512]{1,0:T(8,128)(2,1)S(1)} %add_convert_fusion.2.refs_2_), channel_id=1, source_target_pairs={{0,12},{1,13},{2,14},{3,15},{4,8},{5,9},{6,10},{7,11},{8,4},{9,5},... | collective-permute-start | bytes 147464 | tf_op jit(solution)/shard_map/ppermute | solution.py:393
  64.9 8.4 %collective-permute-start.8 = (bf16[48,512]{1,0:T(8,128)(2,1)S(1)}, bf16[48,512]{1,0:T(8,128)(2,1)S(1)}, u32[]{:S(2)}, u32[]{:S(2)}) collective-permute-start(bf16[48,512]{1,0:T(8,128)(2,1)S(1)} %add_convert_fusion.2.refs_2_), channel_id=1, source_target_pairs={{0,8},{1,9},{2,10},{3,11},{4,12},{5,13},{6,14},{7,15},{8,0},{9,1},... | collective-permute-start | bytes 147464 | tf_op jit(solution)/shard_map/ppermute | solution.py:393
  65.9 7.4 %collective-permute-start.7 = (bf16[48,512]{1,0:T(8,128)(2,1)S(1)}, bf16[48,512]{1,0:T(8,128)(2,1)S(1)}, u32[]{:S(2)}, u32[]{:S(2)}) collective-permute-start(bf16[48,512]{1,0:T(8,128)(2,1)S(1)} %add_convert_fusion.2.refs_2_), channel_id=1, source_target_pairs={{0,4},{1,5},{2,6},{3,7},{4,0},{5,1},{6,2},{7,3},{8,12},{9,13},{10,... | collective-permute-start | bytes 147464 | tf_op jit(solution)/shard_map/ppermute | solution.py:393
  125.9 1.3 collective-permute-start.11
  127.2 5.3 %collective-permute-start.14 = (bf16[48,512]{1,0:T(8,128)(2,1)S(1)}, bf16[48,512]{1,0:T(8,128)(2,1)S(1)}, u32[]{:S(2)}, u32[]{:S(2)}) collective-permute-start(bf16[48,512]{1,0:T(8,128)(2,1)S(1)} %add_convert_fusion.1), channel_id=1, source_target_pairs={{0,18},{1,19},{2,16},{3,17},{4,22},{5,23},{6,20},{7,21},{8,26},{9,... | collective-permute-start | bytes 147464 | tf_op jit(solution)/shard_map/ppermute | solution.py:393
  127.3 5.2 %collective-permute-start.13 = (bf16[48,512]{1,0:T(8,128)(2,1)S(1)}, bf16[48,512]{1,0:T(8,128)(2,1)S(1)}, u32[]{:S(2)}, u32[]{:S(2)}) collective-permute-start(bf16[48,512]{1,0:T(8,128)(2,1)S(1)} %add_convert_fusion.1), channel_id=1, source_target_pairs={{0,16},{1,17},{2,18},{3,19},{4,20},{5,21},{6,22},{7,23},{8,24},{9,... | collective-permute-start | bytes 147464 | tf_op jit(solution)/shard_map/ppermute | solution.py:393
  128.4 4.4 %collective-permute-start.12 = (bf16[48,512]{1,0:T(8,128)(2,1)S(1)}, bf16[48,512]{1,0:T(8,128)(2,1)S(1)}, u32[]{:S(2)}, u32[]{:S(2)}) collective-permute-start(bf16[48,512]{1,0:T(8,128)(2,1)S(1)} %add_convert_fusion.1), channel_id=1, source_target_pairs={{0,2},{1,3},{2,0},{3,1},{4,6},{5,7},{6,4},{7,5},{8,10},{9,11},{10,... | collective-permute-start | bytes 147464 | tf_op jit(solution)/shard_map/ppermute | solution.py:393
  130.8 11.3 %collective-permute-start.10 = (bf16[64,512]{1,0:T(8,128)(2,1)S(1)}, bf16[64,512]{1,0:T(8,128)(2,1)S(1)}, u32[]{:S(2)}, u32[]{:S(2)}) collective-permute-start(bf16[64,512]{1,0:T(8,128)(2,1)S(1)} %get-tuple-element.29), channel_id=1, source_target_pairs={{0,1},{1,2},{2,3},{3,4},{4,5},{5,6},{6,7},{7,8},{8,9},{9,10},{10,1... | collective-permute-start | bytes 196616 | tf_op jit(solution)/shard_map/ppermute | solution.py:389
  132.9 11.9 %collective-permute-start.17 = (bf16[48,512]{1,0:T(8,128)(2,1)S(1)}, bf16[48,512]{1,0:T(8,128)(2,1)S(1)}, u32[]{:S(2)}, u32[]{:S(2)}) collective-permute-start(bf16[48,512]{1,0:T(8,128)(2,1)S(1)} %add_convert_fusion.refs_1_), channel_id=1, source_target_pairs={{0,12},{1,13},{2,14},{3,15},{4,8},{5,9},{6,10},{7,11},{8,4},{9,5},... | collective-permute-start | bytes 147464 | tf_op jit(solution)/shard_map/ppermute | solution.py:393
  139.7 8.1 %collective-permute-start.16 = (bf16[48,512]{1,0:T(8,128)(2,1)S(1)}, bf16[48,512]{1,0:T(8,128)(2,1)S(1)}, u32[]{:S(2)}, u32[]{:S(2)}) collective-permute-start(bf16[48,512]{1,0:T(8,128)(2,1)S(1)} %add_convert_fusion.refs_1_), channel_id=1, source_target_pairs={{0,8},{1,9},{2,10},{3,11},{4,12},{5,13},{6,14},{7,15},{8,0},{9,1},... | collective-permute-start | bytes 147464 | tf_op jit(solution)/shard_map/ppermute | solution.py:393
  140.4 7.4 %collective-permute-start.15 = (bf16[48,512]{1,0:T(8,128)(2,1)S(1)}, bf16[48,512]{1,0:T(8,128)(2,1)S(1)}, u32[]{:S(2)}, u32[]{:S(2)}) collective-permute-start(bf16[48,512]{1,0:T(8,128)(2,1)S(1)} %add_convert_fusion.refs_1_), channel_id=1, source_target_pairs={{0,4},{1,5},{2,6},{3,7},{4,0},{5,1},{6,2},{7,3},{8,12},{9,13},{10,... | collective-permute-start | bytes 147464 | tf_op jit(solution)/shard_map/ppermute | solution.py:393

commit v2 on v1

--- a/solution.py
+++ b/solution.py
@@ -41,9 +41,10 @@
     return c, s
 
 
-def prepare_kernel(c_ref, s_ref, amp_ref, m1_ref, m2_ref):
-    c = c_ref[...].astype(BF)
-    s = s_ref[...]
+def prepare_kernel(tab_ref, amp_ref, amp_out, m1_ref, m2_ref):
+    amp_out[...] = amp_ref[...]
+    c = tab_ref[0].astype(BF)
+    s = tab_ref[1]
     for table, sign in ((m1_ref, -1.0), (m2_ref, 1.0)):
         table[:PS, :PS] = c
         table[:PS, PS:] = (sign * s).astype(BF)
@@ -53,16 +54,16 @@
 
 def prepare(amps):
     table = jax.ShapeDtypeStruct((2 * PS, 2 * PS), BF)
-    rounded = [jnp.asarray(t.astype(jnp.bfloat16).astype(np.float32)) for t in tables()]
+    rounded = jnp.asarray(np.stack(tables()).astype(jnp.bfloat16).astype(np.float32))
     return pl.pallas_call(
         prepare_kernel,
-        out_shape=[table, table],
-        in_specs=[vmem()] * 3,
-        out_specs=[vmem()] * 2,
+        out_shape=[jax.ShapeDtypeStruct(amps.shape, BF), table, table],
+        in_specs=[vmem()] * 2,
+        out_specs=[vmem()] * 3,
         compiler_params=params(8),
         cost_estimate=pl.CostEstimate(flops=0, bytes_accessed=8 << 20, transcendentals=0),
         name="prepare",
-    )(*rounded, amps)
+    )(rounded, amps)
 
 
 def pattern_kernel(first, pos_ref, cnt_ref, obj_ref, halo_ref, probe_ref, amp_ref, extra_ref, m1, m2, *rest):
@@ -409,8 +410,7 @@
 def on_device(object_field, probe, amplitudes, positions, counts):
     pos = positions[0, 0].T
     cnt = counts[0, 0].reshape(1)
-    amps = amplitudes[0, 0]
-    tabs = prepare(amps)
+    amps, *tabs = prepare(amplitudes[0, 0])
     halo = shifted(object_field.astype(BF), -1)
     live = lax.broadcasted_iota(jnp.int32, (CAP,), 0) < cnt
     row = jnp.concatenate([jnp.where(live, pos[0] - lax.axis_index("tile") * TH + 1, 0), pos[1], cnt])

time: 166 us -> 163 us (0.982)
  Pallas kernels: 27.7 us -> 20.4 us
  starting transfers between devices: 30.6 us -> 35.7 us
  waiting for transfers between devices: 17.4 us -> 21.2 us
  blocking collectives: 82.2 us -> 80.2 us
    pallas_call x2, Pallas kernels: 20.4 us -> 14 us  [patterns(): pl.pallas_call(functools.partial(pattern_kernel, first), out_shape=out, i...]
    ppermute x4, starting transfers between devices: 7.55 us -> 11.4 us  [shifted(): lax.ppermute(block, 'tile', [(i, (i + distance) % NT) for i in range(NT)])]
    ppermute x14, waiting for transfers between devices: 11.9 us -> 14.8 us  [swapped(): return lax.ppermute(block, 'tile', [(i, i ^ bits) for i in range(NT)])]
    all_to_all x4, blocking collectives: 82.2 us -> 80.2 us  [exchange(): return lax.all_to_all(blocks, 'scan', 0, 0, tiled=True)]
  transfers between devices with their start and end apart: 18 -> 18, of which waited for: 9 -> 11; matrix products, arithmetic and copies ran while one was open for 1% -> 0% of each run, Pallas kernels for 3% -> 3%
where the time goes in v2:
time: 163 us
  blocking collectives  80.2 us (49%)
  starting transfers between devices  35.7 us (22%)
  waiting for transfers between devices  21.2 us (13%)
  Pallas kernels  20.4 us (13%)
  local copies, waits for them, and re-layouts  2.48 us (2%)
  other arithmetic  1.67 us (1%)
    all_to_all x4, blocking collectives, exchange(): return lax.all_to_all(blocks, 'scan', 0, 0, tiled=True)  80.2 us
    ppermute x14, starting transfers between devices, swapped(): return lax.ppermute(block, 'tile', [(i, i ^ bits) for i in range(NT)])  24.3 us
    ppermute x14, waiting for transfers between devices, swapped(): return lax.ppermute(block, 'tile', [(i, i ^ bits) for i in range(NT)])  14.8 us
    pallas_call x2, Pallas kernels, patterns(): pl.pallas_call(functools.partial(pattern_kernel, first), out_shape=out, i...  14 us
    ppermute x4, starting transfers between devices, shifted(): lax.ppermute(block, 'tile', [(i, (i + distance) % NT) for i in range(NT)])  11.4 us
    ppermute x4, waiting for transfers between devices, shifted(): lax.ppermute(block, 'tile', [(i, (i + distance) % NT) for i in range(NT)])  6.43 us
    pallas_call x2, Pallas kernels, own_step(): pl.pallas_call(own_kernel, out_shape=jax.ShapeDtypeStruct((2 * SR, OW), B...  4.31 us
  transfers between devices with their start and end apart: 18, of which 11 were waited for; matrix products, arithmetic and copies ran while one was open for 0% of the time, Pallas kernels for 3%

profile of v2, /device:TPU:8, one launch (start us, length us, event | category | flops | bytes accessed | tf_op | source)
XLA Modules:
  0.0 163.3 jit_solution(17648921262353709007)
XLA Ops:
  0.7 1.4 convert_element_type.62
  2.1 5.3 %collective-permute-start = (bf16[2,256,512]{2,1,0:T(8,128)(2,1)S(1)}, bf16[2,256,512]{2,1,0:T(8,128)(2,1)S(1)}, u32[]{:S(2)}, u32[]{:S(2)}) collective-permute-start(bf16[2,256,512]{2,1,0:T(8,128)(2,1)S(1)} %convert_element_type.62), channel_id=1, source_target_pairs={{0,31},{1,0},{2,1},{3,2},{4,3},{5,4},{6,5},{7,6},{8,7},{9,8},{10,9... | collective-permute-start | bytes 1572872 | tf_op jit(solution)/shard_map/ppermute | solution.py:390
  8.2 1.4 copy-done.2
  9.6 1.0 copy-done.3
  10.8 3.2 %collective-permute-done.halo_ref = bf16[2,256,512]{2,1,0:T(8,128)(2,1)S(1)} collective-permute-done((bf16[2,256,512]{2,1,0:T(8,128)(2,1)S(1)}, bf16[2,256,512]{2,1,0:T(8,128)(2,1)S(1)}, u32[]{:S(2)}, u32[]{:S(2)}) %collective-permute-start) | collective-permute-done | bytes 524320 | tf_op jit(solution)/shard_map/ppermute | solution.py:390
  14.0 6.8 %patterns.2 = bf16[8,192,512]{2,1,0:T(8,128)(2,1)S(1)} custom-call(s32[2,12]{1,0:T(2,128)S(1)} %bitcast.17, s32[1]{0:T(128)} %bitcast.11.cnt_ref, f32[2,256,512]{2,1,0:T(8,128)S(1)} %copy-done, bf16[2,256,512]{2,1,0:T(8,128)(2,1)S(1)} %collective-permute-done.halo_ref, f32[2,256,256]{2,1,0:T(8,128)S(1)} %copy-done.1, ...), custom_call_target="tpu_custom_call" | custom-call | tf_op jit(solution)/shard_map/patterns/pallas_call | solution.py:214
  20.9 22.7 %all_to_all.20.recv_ref = bf16[8,192,512]{2,1,0:T(8,128)(2,1)S(1)} all-to-all(bf16[8,192,512]{2,1,0:T(8,128)(2,1)S(1)} %patterns.2), channel_id=1, replica_groups=mesh['scan'=8,'tile'=32] {'scan'}, dimensions={0} | all-to-all | bytes 3145728 | tf_op jit(solution)/shard_map/all_to_all | solution.py:407
  44.3 0.7 collective-permute-done.1
  45.1 1.5 collective-permute-start.4
  47.0 1.6 %collective-permute-start.2 = (bf16[48,512]{1,0:T(8,128)(2,1)S(1)}, bf16[48,512]{1,0:T(8,128)(2,1)S(1)}, u32[]{:S(2)}, u32[]{:S(2)}) collective-permute-start(bf16[48,512]{1,0:T(8,128)(2,1)S(1)} %add_convert_fusion.3), channel_id=1, source_target_pairs={{0,2},{1,3},{2,0},{3,1},{4,6},{5,7},{6,4},{7,5},{8,10},{9,11},{10,... | collective-permute-start | bytes 147464 | tf_op jit(solution)/shard_map/ppermute | solution.py:394
  48.6 3.2 %collective-permute-done.5.up_ref = bf16[80,512]{1,0:T(8,128)(2,1)S(1)} collective-permute-done((bf16[80,512]{1,0:T(8,128)(2,1)S(1)}, bf16[80,512]{1,0:T(8,128)(2,1)S(1)}, u32[]{:S(2)}, u32[]{:S(2)}) %collective-permute-start.5) | collective-permute-done | bytes 81952 | tf_op jit(solution)/shard_map/ppermute | solution.py:390
  51.9 2.2 %own_step.2.refs_0_ = bf16[64,512]{1,0:T(8,128)(2,1)S(1)} custom-call(s32[16,25]{1,0:T(8,128)S(1)} %maximum_convert_fusion.pos_ref, f32[2,256,256]{2,1,0:T(8,128)S(1)} %copy-done.1, f32[64,512]{1,0:T(8,128)S(1)} %get-tuple-element.24.own_ref, bf16[80,512]{1,0:T(8,128)(2,1)S(1)} %collective-permute-done.5.up_ref), custom_call_target="tpu_custom_call" | custom-call | tf_op jit(solution)/shard_map/own_step/pallas_call | solution.py:318
  54.1 5.7 %collective-permute-start.6 = (bf16[64,512]{1,0:T(8,128)(2,1)S(1)}, bf16[64,512]{1,0:T(8,128)(2,1)S(1)}, u32[]{:S(2)}, u32[]{:S(2)}) collective-permute-start(bf16[64,512]{1,0:T(8,128)(2,1)S(1)} %own_step.2.refs_0_), channel_id=1, source_target_pairs={{0,31},{1,0},{2,1},{3,2},{4,3},{5,4},{6,5},{7,6},{8,7},{9,8},{10,9... | collective-permute-start | bytes 196616 | tf_op jit(solution)/shard_map/ppermute | solution.py:390
  59.8 2.6 %collective-permute-start.9 = (bf16[48,512]{1,0:T(8,128)(2,1)S(1)}, bf16[48,512]{1,0:T(8,128)(2,1)S(1)}, u32[]{:S(2)}, u32[]{:S(2)}) collective-permute-start(bf16[48,512]{1,0:T(8,128)(2,1)S(1)} %add_convert_fusion.2.refs_2_), channel_id=1, source_target_pairs={{0,12},{1,13},{2,14},{3,15},{4,8},{5,9},{6,10},{7,11},{8,4},{9,5},... | collective-permute-start | bytes 147464 | tf_op jit(solution)/shard_map/ppermute | solution.py:394
  62.4 1.2 collective-permute-start.8
  63.6 2.7 %collective-permute-start.7 = (bf16[48,512]{1,0:T(8,128)(2,1)S(1)}, bf16[48,512]{1,0:T(8,128)(2,1)S(1)}, u32[]{:S(2)}, u32[]{:S(2)}) collective-permute-start(bf16[48,512]{1,0:T(8,128)(2,1)S(1)} %add_convert_fusion.2.refs_2_), channel_id=1, source_target_pairs={{0,4},{1,5},{2,6},{3,7},{4,0},{5,1},{6,2},{7,3},{8,12},{9,13},{10,... | collective-permute-start | bytes 147464 | tf_op jit(solution)/shard_map/ppermute | solution.py:394
  66.8 4.4 %collective-permute-done.8.refs_4_ = bf16[48,512]{1,0:T(8,128)(2,1)S(1)} collective-permute-done((bf16[48,512]{1,0:T(8,128)(2,1)S(1)}, bf16[48,512]{1,0:T(8,128)(2,1)S(1)}, u32[]{:S(2)}, u32[]{:S(2)}) %collective-permute-start.8) | collective-permute-done | bytes 49184 | tf_op jit(solution)/shard_map/ppermute | solution.py:394
  71.3 22.1 %all_to_all.21.extra_ref = bf16[8,160,512]{2,1,0:T(8,128)(2,1)S(1)} all-to-all(bf16[8,160,512]{2,1,0:T(8,128)(2,1)S(1)} %spread.2), channel_id=1, replica_groups=mesh['scan'=8,'tile'=32] {'scan'}, dimensions={0} | all-to-all | bytes 2621440 | tf_op jit(solution)/shard_map/all_to_all | solution.py:407
  93.3 7.1 %patterns.3 = (bf16[8,176,512]{2,1,0:T(8,128)(2,1)S(1)}, f32[2,256,512]{2,1,0:T(8,128)S(1)}, f32[2,256,256]{2,1,0:T(8,128)S(1)}) custom-call(s32[2,12]{1,0:T(2,128)S(1)} %bitcast.18, s32[1]{0:T(128)} %bitcast.12.cnt_ref, f32[2,256,512]{2,1,0:T(8,128)S(1)} %copy-done, bf16[2,256,512]{2,1,0:T(8,128)(2,1)S(1)} %collective-permute-done.halo_ref, ...), custom_call_target="tpu_custom_call" | custom-call | tf_op jit(solution)/shard_map/patterns/pallas_call | solution.py:214
  100.5 19.3 %all_to_all.22.recv_ref = bf16[8,176,512]{2,1,0:T(8,128)(2,1)S(1)} all-to-all(bf16[8,176,512]{2,1,0:T(8,128)(2,1)S(1)} %get-tuple-element.29), channel_id=1, replica_groups=mesh['scan'=8,'tile'=32] {'scan'}, dimensions={0} | all-to-all | bytes 2883584 | tf_op jit(solution)/shard_map/all_to_all | solution.py:407
  120.1 1.2 collective-permute-done.11
  121.3 2.2 %collective-permute-start.14 = (bf16[48,512]{1,0:T(8,128)(2,1)S(1)}, bf16[48,512]{1,0:T(8,128)(2,1)S(1)}, u32[]{:S(2)}, u32[]{:S(2)}) collective-permute-start(bf16[48,512]{1,0:T(8,128)(2,1)S(1)} %add_convert_fusion.1), channel_id=1, source_target_pairs={{0,18},{1,19},{2,16},{3,17},{4,22},{5,23},{6,20},{7,21},{8,26},{9,... | collective-permute-start | bytes 147464 | tf_op jit(solution)/shard_map/ppermute | solution.py:394
  123.5 2.2 %collective-permute-start.13 = (bf16[48,512]{1,0:T(8,128)(2,1)S(1)}, bf16[48,512]{1,0:T(8,128)(2,1)S(1)}, u32[]{:S(2)}, u32[]{:S(2)}) collective-permute-start(bf16[48,512]{1,0:T(8,128)(2,1)S(1)} %add_convert_fusion.1), channel_id=1, source_target_pairs={{0,16},{1,17},{2,18},{3,19},{4,20},{5,21},{6,22},{7,23},{8,24},{9,... | collective-permute-start | bytes 147464 | tf_op jit(solution)/shard_map/ppermute | solution.py:394
  126.4 1.4 collective-permute-done.13
  127.8 2.0 %collective-permute-done.12 = bf16[48,512]{1,0:T(8,128)(2,1)S(1)} collective-permute-done((bf16[48,512]{1,0:T(8,128)(2,1)S(1)}, bf16[48,512]{1,0:T(8,128)(2,1)S(1)}, u32[]{:S(2)}, u32[]{:S(2)}) %collective-permute-start.12) | collective-permute-done | bytes 49184 | tf_op jit(solution)/shard_map/ppermute | solution.py:394
  129.8 5.4 %collective-permute-start.17 = (bf16[48,512]{1,0:T(8,128)(2,1)S(1)}, bf16[48,512]{1,0:T(8,128)(2,1)S(1)}, u32[]{:S(2)}, u32[]{:S(2)}) collective-permute-start(bf16[48,512]{1,0:T(8,128)(2,1)S(1)} %add_convert_fusion.refs_1_), channel_id=1, source_target_pairs={{0,12},{1,13},{2,14},{3,15},{4,8},{5,9},{6,10},{7,11},{8,4},{9,5},... | collective-permute-start | bytes 147464 | tf_op jit(solution)/shard_map/ppermute | solution.py:394
  135.2 4.2 %collective-permute-start.16 = (bf16[48,512]{1,0:T(8,128)(2,1)S(1)}, bf16[48,512]{1,0:T(8,128)(2,1)S(1)}, u32[]{:S(2)}, u32[]{:S(2)}) collective-permute-start(bf16[48,512]{1,0:T(8,128)(2,1)S(1)} %add_convert_fusion.refs_1_), channel_id=1, source_target_pairs={{0,8},{1,9},{2,10},{3,11},{4,12},{5,13},{6,14},{7,15},{8,0},{9,1},... | collective-permute-start | bytes 147464 | tf_op jit(solution)/shard_map/ppermute | solution.py:394
  139.5 2.2 %own_step.3.refs_0_ = bf16[64,512]{1,0:T(8,128)(2,1)S(1)} custom-call(s32[16,25]{1,0:T(8,128)S(1)} %maximum_convert_fusion.pos_ref, f32[2,256,256]{2,1,0:T(8,128)S(1)} %get-tuple-element.28.probe_ref, f32[64,512]{1,0:T(8,128)S(1)} %get-tuple-element.30.own_ref, bf16[64,512]{1,0:T(8,128)(2,1)S(1)} %collective-permute-done.10.up_ref), custom_call_target="tpu_custom_call" | custom-call | tf_op jit(solution)/shard_map/own_step/pallas_call | solution.py:318
  141.7 3.0 %collective-permute-done.16.refs_3_ = bf16[48,512]{1,0:T(8,128)(2,1)S(1)} collective-permute-done((bf16[48,512]{1,0:T(8,128)(2,1)S(1)}, bf16[48,512]{1,0:T(8,128)(2,1)S(1)}, u32[]{:S(2)}, u32[]{:S(2)}) %collective-permute-start.16) | collective-permute-done | bytes 49184 | tf_op jit(solution)/shard_map/ppermute | solution.py:394
  144.7 0.9 collective-permute-done.15.refs_2_
  145.6 16.2 %all_to_all.23.recv_ref = bf16[8,112,512]{2,1,0:T(8,128)(2,1)S(1)} all-to-all(bf16[8,112,512]{2,1,0:T(8,128)(2,1)S(1)} %spread.3), channel_id=1, replica_groups=mesh['scan'=8,'tile'=32] {'scan'}, dimensions={0} | all-to-all | bytes 1835008 | tf_op jit(solution)/shard_map/all_to_all | solution.py:407
  161.8 1.4 final.1
  (42 shorter events, 3.3 us)
Async XLA Ops:
  0.6 13.4 %copy-start = (f32[2,256,512]{2,1,0:T(8,128)S(1)}, f32[2,256,512]{2,1,0:T(8,128)}, u32[]{:S(2)}) copy-start(f32[2,256,512]{2,1,0:T(8,128)} %obj_ref.3) | copy-start | bytes 3145732
  0.6 7.4 %copy-start.4 = (s32[1,1,12,2]{2,3,1,0:T(2,128)S(1)}, s32[1,1,12,2]{2,3,1,0:T(2,128)}, u32[]{:S(2)}) copy-start(s32[1,1,12,2]{2,3,1,0:T(2,128)} %param.9) | copy-start | bytes 292
  0.7 13.4 %copy-start.1 = (f32[2,256,256]{2,1,0:T(8,128)S(1)}, f32[2,256,256]{2,1,0:T(8,128)}, u32[]{:S(2)}) copy-start(f32[2,256,256]{2,1,0:T(8,128)} %probe_ref.5) | copy-start | bytes 1572868
  2.1 12.0 %collective-permute-start = (bf16[2,256,512]{2,1,0:T(8,128)(2,1)S(1)}, bf16[2,256,512]{2,1,0:T(8,128)(2,1)S(1)}, u32[]{:S(2)}, u32[]{:S(2)}) collective-permute-start(bf16[2,256,512]{2,1,0:T(8,128)(2,1)S(1)} %convert_element_type.62), channel_id=1, source_target_pairs={{0,31},{1,0},{2,1},{3,2},{4,3},{5,4},{6,5},{7,6},{8,7},{9,8},{10,9... | collective-permute-start | bytes 1572872 | tf_op jit(solution)/shard_map/ppermute | solution.py:390
  8.2 1.4 copy-start.2
  9.6 1.0 copy-start.3
  43.7 1.3 collective-permute-start.1
  43.8 8.0 %collective-permute-start.5 = (bf16[80,512]{1,0:T(8,128)(2,1)S(1)}, bf16[80,512]{1,0:T(8,128)(2,1)S(1)}, u32[]{:S(2)}, u32[]{:S(2)}) collective-permute-start(bf16[80,512]{1,0:T(8,128)(2,1)S(1)} %get-tuple-element.22), channel_id=1, source_target_pairs={{0,1},{1,2},{2,3},{3,4},{4,5},{5,6},{6,7},{7,8},{8,9},{9,10},{10,1... | collective-permute-start | bytes 245768 | tf_op jit(solution)/shard_map/ppermute | solution.py:390
  45.1 9.0 %collective-permute-start.4 = (bf16[48,512]{1,0:T(8,128)(2,1)S(1)}, bf16[48,512]{1,0:T(8,128)(2,1)S(1)}, u32[]{:S(2)}, u32[]{:S(2)}) collective-permute-start(bf16[48,512]{1,0:T(8,128)(2,1)S(1)} %add_convert_fusion.3), channel_id=1, source_target_pairs={{0,18},{1,19},{2,16},{3,17},{4,22},{5,23},{6,20},{7,21},{8,26},{9,... | collective-permute-start | bytes 147464 | tf_op jit(solution)/shard_map/ppermute | solution.py:394
  46.5 7.5 %collective-permute-start.3 = (bf16[48,512]{1,0:T(8,128)(2,1)S(1)}, bf16[48,512]{1,0:T(8,128)(2,1)S(1)}, u32[]{:S(2)}, u32[]{:S(2)}) collective-permute-start(bf16[48,512]{1,0:T(8,128)(2,1)S(1)} %add_convert_fusion.3), channel_id=1, source_target_pairs={{0,16},{1,17},{2,18},{3,19},{4,20},{5,21},{6,22},{7,23},{8,24},{9,... | collective-permute-start | bytes 147464 | tf_op jit(solution)/shard_map/ppermute | solution.py:394
  47.0 7.1 %collective-permute-start.2 = (bf16[48,512]{1,0:T(8,128)(2,1)S(1)}, bf16[48,512]{1,0:T(8,128)(2,1)S(1)}, u32[]{:S(2)}, u32[]{:S(2)}) collective-permute-start(bf16[48,512]{1,0:T(8,128)(2,1)S(1)} %add_convert_fusion.3), channel_id=1, source_target_pairs={{0,2},{1,3},{2,0},{3,1},{4,6},{5,7},{6,4},{7,5},{8,10},{9,11},{10,... | collective-permute-start | bytes 147464 | tf_op jit(solution)/shard_map/ppermute | solution.py:394
  54.1 17.1 %collective-permute-start.6 = (bf16[64,512]{1,0:T(8,128)(2,1)S(1)}, bf16[64,512]{1,0:T(8,128)(2,1)S(1)}, u32[]{:S(2)}, u32[]{:S(2)}) collective-permute-start(bf16[64,512]{1,0:T(8,128)(2,1)S(1)} %own_step.2.refs_0_), channel_id=1, source_target_pairs={{0,31},{1,0},{2,1},{3,2},{4,3},{5,4},{6,5},{7,6},{8,7},{9,8},{10,9... | collective-permute-start | bytes 196616 | tf_op jit(solution)/shard_map/ppermute | solution.py:390
  59.8 7.0 %collective-permute-start.9 = (bf16[48,512]{1,0:T(8,128)(2,1)S(1)}, bf16[48,512]{1,0:T(8,128)(2,1)S(1)}, u32[]{:S(2)}, u32[]{:S(2)}) collective-permute-start(bf16[48,512]{1,0:T(8,128)(2,1)S(1)} %add_convert_fusion.2.refs_2_), channel_id=1, source_target_pairs={{0,12},{1,13},{2,14},{3,15},{4,8},{5,9},{6,10},{7,11},{8,4},{9,5},... | collective-permute-start | bytes 147464 | tf_op jit(solution)/shard_map/ppermute | solution.py:394
  62.4 8.8 %collective-permute-start.8 = (bf16[48,512]{1,0:T(8,128)(2,1)S(1)}, bf16[48,512]{1,0:T(8,128)(2,1)S(1)}, u32[]{:S(2)}, u32[]{:S(2)}) collective-permute-start(bf16[48,512]{1,0:T(8,128)(2,1)S(1)} %add_convert_fusion.2.refs_2_), channel_id=1, source_target_pairs={{0,8},{1,9},{2,10},{3,11},{4,12},{5,13},{6,14},{7,15},{8,0},{9,1},... | collective-permute-start | bytes 147464 | tf_op jit(solution)/shard_map/ppermute | solution.py:394
  63.6 7.6 %collective-permute-start.7 = (bf16[48,512]{1,0:T(8,128)(2,1)S(1)}, bf16[48,512]{1,0:T(8,128)(2,1)S(1)}, u32[]{:S(2)}, u32[]{:S(2)}) collective-permute-start(bf16[48,512]{1,0:T(8,128)(2,1)S(1)} %add_convert_fusion.2.refs_2_), channel_id=1, source_target_pairs={{0,4},{1,5},{2,6},{3,7},{4,0},{5,1},{6,2},{7,3},{8,12},{9,13},{10,... | collective-permute-start | bytes 147464 | tf_op jit(solution)/shard_map/ppermute | solution.py:394
  120.0 1.3 collective-permute-start.11
  121.3 5.1 %collective-permute-start.14 = (bf16[48,512]{1,0:T(8,128)(2,1)S(1)}, bf16[48,512]{1,0:T(8,128)(2,1)S(1)}, u32[]{:S(2)}, u32[]{:S(2)}) collective-permute-start(bf16[48,512]{1,0:T(8,128)(2,1)S(1)} %add_convert_fusion.1), channel_id=1, source_target_pairs={{0,18},{1,19},{2,16},{3,17},{4,22},{5,23},{6,20},{7,21},{8,26},{9,... | collective-permute-start | bytes 147464 | tf_op jit(solution)/shard_map/ppermute | solution.py:394
  123.5 4.3 %collective-permute-start.13 = (bf16[48,512]{1,0:T(8,128)(2,1)S(1)}, bf16[48,512]{1,0:T(8,128)(2,1)S(1)}, u32[]{:S(2)}, u32[]{:S(2)}) collective-permute-start(bf16[48,512]{1,0:T(8,128)(2,1)S(1)} %add_convert_fusion.1), channel_id=1, source_target_pairs={{0,16},{1,17},{2,18},{3,19},{4,20},{5,21},{6,22},{7,23},{8,24},{9,... | collective-permute-start | bytes 147464 | tf_op jit(solution)/shard_map/ppermute | solution.py:394
  125.7 4.1 %collective-permute-start.12 = (bf16[48,512]{1,0:T(8,128)(2,1)S(1)}, bf16[48,512]{1,0:T(8,128)(2,1)S(1)}, u32[]{:S(2)}, u32[]{:S(2)}) collective-permute-start(bf16[48,512]{1,0:T(8,128)(2,1)S(1)} %add_convert_fusion.1), channel_id=1, source_target_pairs={{0,2},{1,3},{2,0},{3,1},{4,6},{5,7},{6,4},{7,5},{8,10},{9,11},{10,... | collective-permute-start | bytes 147464 | tf_op jit(solution)/shard_map/ppermute | solution.py:394
  125.7 13.8 %collective-permute-start.10 = (bf16[64,512]{1,0:T(8,128)(2,1)S(1)}, bf16[64,512]{1,0:T(8,128)(2,1)S(1)}, u32[]{:S(2)}, u32[]{:S(2)}) collective-permute-start(bf16[64,512]{1,0:T(8,128)(2,1)S(1)} %get-tuple-element.31), channel_id=1, source_target_pairs={{0,1},{1,2},{2,3},{3,4},{4,5},{5,6},{6,7},{7,8},{8,9},{9,10},{10,1... | collective-permute-start | bytes 196616 | tf_op jit(solution)/shard_map/ppermute | solution.py:390
  129.8 11.8 %collective-permute-start.17 = (bf16[48,512]{1,0:T(8,128)(2,1)S(1)}, bf16[48,512]{1,0:T(8,128)(2,1)S(1)}, u32[]{:S(2)}, u32[]{:S(2)}) collective-permute-start(bf16[48,512]{1,0:T(8,128)(2,1)S(1)} %add_convert_fusion.refs_1_), channel_id=1, source_target_pairs={{0,12},{1,13},{2,14},{3,15},{4,8},{5,9},{6,10},{7,11},{8,4},{9,5},... | collective-permute-start | bytes 147464 | tf_op jit(solution)/shard_map/ppermute | solution.py:394
  135.2 9.4 %collective-permute-start.16 = (bf16[48,512]{1,0:T(8,128)(2,1)S(1)}, bf16[48,512]{1,0:T(8,128)(2,1)S(1)}, u32[]{:S(2)}, u32[]{:S(2)}) collective-permute-start(bf16[48,512]{1,0:T(8,128)(2,1)S(1)} %add_convert_fusion.refs_1_), channel_id=1, source_target_pairs={{0,8},{1,9},{2,10},{3,11},{4,12},{5,13},{6,14},{7,15},{8,0},{9,1},... | collective-permute-start | bytes 147464 | tf_op jit(solution)/shard_map/ppermute | solution.py:394
  139.5 6.0 %collective-permute-start.15 = (bf16[48,512]{1,0:T(8,128)(2,1)S(1)}, bf16[48,512]{1,0:T(8,128)(2,1)S(1)}, u32[]{:S(2)}, u32[]{:S(2)}) collective-permute-start(bf16[48,512]{1,0:T(8,128)(2,1)S(1)} %add_convert_fusion.refs_1_), channel_id=1, source_target_pairs={{0,4},{1,5},{2,6},{3,7},{4,0},{5,1},{6,2},{7,3},{8,12},{9,13},{10,... | collective-permute-start | bytes 147464 | tf_op jit(solution)/shard_map/ppermute | solution.py:394

commit v3 on v2

--- a/solution.py
+++ b/solution.py
@@ -21,7 +21,7 @@
 GRANT = 20
 SOME = 4
 UN = 8
-PAIR = 3
+PAIR = 4
 FLOOR2 = 0.25
 REG = 1.0
 
@@ -426,7 +426,7 @@
     swaps = [swapped(part, d) for d in (2, 16, 18)]
     around = jnp.concatenate([up[2 * SR :, :coded][:NS].astype(F32), tile_pos[:NS, :coded]], 0).astype(jnp.int32)
     delta = own_step(around, probe, own, up)
-    part, delta = lax.optimization_barrier((four(part, swaps), delta))
+    part = four(part, swaps)
     swaps = [swapped(part, d) for d in (4, 8, 12)]
     recv = exchange(spread(False, delta, shifted(delta, -1), part, *swaps))
     send, object_field, probe = patterns(pos, cnt, object_field, halo, probe, amps, tabs, recv=recv)

time: 163 us -> 165 us (1.012)
  waiting for transfers between devices: 21.2 us -> 14.5 us
  Pallas kernels: 20.4 us -> 25.9 us
  blocking collectives: 80.2 us -> 82.8 us
    ppermute x14, waiting for transfers between devices: 14.8 us -> 8.64 us  [swapped(): return lax.ppermute(block, 'tile', [(i, i ^ bits) for i in range(NT)])]
    ppermute x4, starting transfers between devices: 11.4 us -> 6.72 us  [shifted(): lax.ppermute(block, 'tile', [(i, (i + distance) % NT) for i in range(NT)])]
    ppermute x14, starting transfers between devices: 24.3 us -> 28.9 us  [swapped(): return lax.ppermute(block, 'tile', [(i, i ^ bits) for i in range(NT)])]
    pallas_call x2, Pallas kernels: 14 us -> 17.5 us  [patterns(): pl.pallas_call(functools.partial(pattern_kernel, first), out_shape=out, i...]
    all_to_all x4, blocking collectives: 80.2 us -> 82.8 us  [exchange(): return lax.all_to_all(blocks, 'scan', 0, 0, tiled=True)]
    pallas_call x2, Pallas kernels: 4.31 us -> 6.24 us  [own_step(): pl.pallas_call(own_kernel, out_shape=jax.ShapeDtypeStruct((2 * SR, OW), B...]
  transfers between devices with their start and end apart: 18 -> 18, of which waited for: 11 -> 7; matrix products, arithmetic and copies ran while one was open for 0% -> 0% of each run, Pallas kernels for 3% -> 4%
where the time goes in v3:
time: 165 us; the launch traced here: 164 us
  blocking collectives  82.8 us (50%)
  starting transfers between devices  35.6 us (22%)
  Pallas kernels  25.9 us (16%)
  waiting for transfers between devices  14.5 us (9%)
  local copies, waits for them, and re-layouts  2.48 us (2%)
  other arithmetic  1.67 us (1%)
    all_to_all x4, blocking collectives, exchange(): return lax.all_to_all(blocks, 'scan', 0, 0, tiled=True)  82.8 us
    ppermute x14, starting transfers between devices, swapped(): return lax.ppermute(block, 'tile', [(i, i ^ bits) for i in range(NT)])  28.9 us
    pallas_call x2, Pallas kernels, patterns(): pl.pallas_call(functools.partial(pattern_kernel, first), out_shape=out, i...  17.5 us
    ppermute x14, waiting for transfers between devices, swapped(): return lax.ppermute(block, 'tile', [(i, i ^ bits) for i in range(NT)])  8.64 us
    ppermute x4, starting transfers between devices, shifted(): lax.ppermute(block, 'tile', [(i, (i + distance) % NT) for i in range(NT)])  6.72 us
    pallas_call x2, Pallas kernels, own_step(): pl.pallas_call(own_kernel, out_shape=jax.ShapeDtypeStruct((2 * SR, OW), B...  6.24 us
    ppermute x4, waiting for transfers between devices, shifted(): lax.ppermute(block, 'tile', [(i, (i + distance) % NT) for i in range(NT)])  5.84 us
  transfers between devices with their start and end apart: 18, of which 7 were waited for; matrix products, arithmetic and copies ran while one was open for 0% of the time, Pallas kernels for 4%

profile of v3, /device:TPU:8, one launch (start us, length us, event | category | flops | bytes accessed | tf_op | source)
XLA Modules:
  0.0 164.5 jit_solution(6726734931559890986)
XLA Ops:
  0.7 1.4 convert_element_type.62
  2.1 5.3 %collective-permute-start = (bf16[2,256,512]{2,1,0:T(8,128)(2,1)S(1)}, bf16[2,256,512]{2,1,0:T(8,128)(2,1)S(1)}, u32[]{:S(2)}, u32[]{:S(2)}) collective-permute-start(bf16[2,256,512]{2,1,0:T(8,128)(2,1)S(1)} %convert_element_type.62), channel_id=1, source_target_pairs={{0,31},{1,0},{2,1},{3,2},{4,3},{5,4},{6,5},{7,6},{8,7},{9,8},{10,9... | collective-permute-start | bytes 1572872 | tf_op jit(solution)/shard_map/ppermute | solution.py:390
  8.2 1.4 copy-done.2
  9.6 1.0 copy-done.3
  10.6 0.2 prepare.1
  10.8 3.2 %collective-permute-done.halo_ref = bf16[2,256,512]{2,1,0:T(8,128)(2,1)S(1)} collective-permute-done((bf16[2,256,512]{2,1,0:T(8,128)(2,1)S(1)}, bf16[2,256,512]{2,1,0:T(8,128)(2,1)S(1)}, u32[]{:S(2)}, u32[]{:S(2)}) %collective-permute-start) | collective-permute-done | bytes 524320 | tf_op jit(solution)/shard_map/ppermute | solution.py:390
  14.0 8.5 %patterns.2 = bf16[8,192,512]{2,1,0:T(8,128)(2,1)S(1)} custom-call(s32[2,12]{1,0:T(2,128)S(1)} %bitcast.17, s32[1]{0:T(128)} %bitcast.11.cnt_ref, f32[2,256,512]{2,1,0:T(8,128)S(1)} %copy-done, bf16[2,256,512]{2,1,0:T(8,128)(2,1)S(1)} %collective-permute-done.halo_ref, f32[2,256,256]{2,1,0:T(8,128)S(1)} %copy-done.1, ...), custom_call_target="tpu_custom_call" | custom-call | tf_op jit(solution)/shard_map/patterns/pallas_call | solution.py:214
  22.6 23.0 %all_to_all.20.recv_ref = bf16[8,192,512]{2,1,0:T(8,128)(2,1)S(1)} all-to-all(bf16[8,192,512]{2,1,0:T(8,128)(2,1)S(1)} %patterns.2), channel_id=1, replica_groups=mesh['scan'=8,'tile'=32] {'scan'}, dimensions={0} | all-to-all | bytes 3145728 | tf_op jit(solution)/shard_map/all_to_all | solution.py:407
  45.6 0.2 sums.2
  45.9 0.5 collective-permute-start.1
  46.4 0.7 collective-permute-done.3
  47.2 0.1 collective-permute-start.6
  47.3 6.5 %collective-permute-start.5 = (bf16[48,512]{1,0:T(8,128)(2,1)S(1)}, bf16[48,512]{1,0:T(8,128)(2,1)S(1)}, u32[]{:S(2)}, u32[]{:S(2)}) collective-permute-start(bf16[48,512]{1,0:T(8,128)(2,1)S(1)} %add_convert_fusion.3), channel_id=1, source_target_pairs={{0,16},{1,17},{2,18},{3,19},{4,20},{5,21},{6,22},{7,23},{8,24},{9,... | collective-permute-start | bytes 147464 | tf_op jit(solution)/shard_map/ppermute | solution.py:394
  53.8 2.6 %collective-permute-done.1.up_ref = bf16[80,512]{1,0:T(8,128)(2,1)S(1)} collective-permute-done((bf16[80,512]{1,0:T(8,128)(2,1)S(1)}, bf16[80,512]{1,0:T(8,128)(2,1)S(1)}, u32[]{:S(2)}, u32[]{:S(2)}) %collective-permute-start.1) | collective-permute-done | bytes 81952 | tf_op jit(solution)/shard_map/ppermute | solution.py:390
  56.4 3.1 %own_step.2.refs_0_ = bf16[64,512]{1,0:T(8,128)(2,1)S(1)} custom-call(s32[16,25]{1,0:T(8,128)S(1)} %maximum_convert_fusion.pos_ref, f32[2,256,256]{2,1,0:T(8,128)S(1)} %copy-done.1, f32[64,512]{1,0:T(8,128)S(1)} %get-tuple-element.21.own_ref, bf16[80,512]{1,0:T(8,128)(2,1)S(1)} %collective-permute-done.1.up_ref), custom_call_target="tpu_custom_call" | custom-call | tf_op jit(solution)/shard_map/own_step/pallas_call | solution.py:318
  59.6 1.0 collective-permute-start.2
  60.6 1.0 collective-permute-start.9
  61.6 2.0 %collective-permute-start.8 = (bf16[48,512]{1,0:T(8,128)(2,1)S(1)}, bf16[48,512]{1,0:T(8,128)(2,1)S(1)}, u32[]{:S(2)}, u32[]{:S(2)}) collective-permute-start(bf16[48,512]{1,0:T(8,128)(2,1)S(1)} %add_convert_fusion.2.refs_2_), channel_id=1, source_target_pairs={{0,8},{1,9},{2,10},{3,11},{4,12},{5,13},{6,14},{7,15},{8,0},{9,1},... | collective-permute-start | bytes 147464 | tf_op jit(solution)/shard_map/ppermute | solution.py:394
  63.5 3.6 %collective-permute-start.7 = (bf16[48,512]{1,0:T(8,128)(2,1)S(1)}, bf16[48,512]{1,0:T(8,128)(2,1)S(1)}, u32[]{:S(2)}, u32[]{:S(2)}) collective-permute-start(bf16[48,512]{1,0:T(8,128)(2,1)S(1)} %add_convert_fusion.2.refs_2_), channel_id=1, source_target_pairs={{0,4},{1,5},{2,6},{3,7},{4,0},{5,1},{6,2},{7,3},{8,12},{9,13},{10,... | collective-permute-start | bytes 147464 | tf_op jit(solution)/shard_map/ppermute | solution.py:394
  67.2 2.6 %collective-permute-done.8.refs_4_ = bf16[48,512]{1,0:T(8,128)(2,1)S(1)} collective-permute-done((bf16[48,512]{1,0:T(8,128)(2,1)S(1)}, bf16[48,512]{1,0:T(8,128)(2,1)S(1)}, u32[]{:S(2)}, u32[]{:S(2)}) %collective-permute-start.8) | collective-permute-done | bytes 49184 | tf_op jit(solution)/shard_map/ppermute | solution.py:394
  69.9 21.9 %all_to_all.21.extra_ref = bf16[8,160,512]{2,1,0:T(8,128)(2,1)S(1)} all-to-all(bf16[8,160,512]{2,1,0:T(8,128)(2,1)S(1)} %spread.2), channel_id=1, replica_groups=mesh['scan'=8,'tile'=32] {'scan'}, dimensions={0} | all-to-all | bytes 2621440 | tf_op jit(solution)/shard_map/all_to_all | solution.py:407
  91.8 8.9 %patterns.3 = (bf16[8,176,512]{2,1,0:T(8,128)(2,1)S(1)}, f32[2,256,512]{2,1,0:T(8,128)S(1)}, f32[2,256,256]{2,1,0:T(8,128)S(1)}) custom-call(s32[2,12]{1,0:T(2,128)S(1)} %bitcast.18, s32[1]{0:T(128)} %bitcast.12.cnt_ref, f32[2,256,512]{2,1,0:T(8,128)S(1)} %copy-done, bf16[2,256,512]{2,1,0:T(8,128)(2,1)S(1)} %collective-permute-done.halo_ref, ...), custom_call_target="tpu_custom_call" | custom-call | tf_op jit(solution)/shard_map/patterns/pallas_call | solution.py:214
  100.7 21.6 %all_to_all.22.recv_ref = bf16[8,176,512]{2,1,0:T(8,128)(2,1)S(1)} all-to-all(bf16[8,176,512]{2,1,0:T(8,128)(2,1)S(1)} %get-tuple-element.25), channel_id=1, replica_groups=mesh['scan'=8,'tile'=32] {'scan'}, dimensions={0} | all-to-all | bytes 2883584 | tf_op jit(solution)/shard_map/all_to_all | solution.py:407
  122.3 0.2 sums.3
  122.6 1.2 collective-permute-done.11
  123.9 8.9 %collective-permute-start.13 = (bf16[48,512]{1,0:T(8,128)(2,1)S(1)}, bf16[48,512]{1,0:T(8,128)(2,1)S(1)}, u32[]{:S(2)}, u32[]{:S(2)}) collective-permute-start(bf16[48,512]{1,0:T(8,128)(2,1)S(1)} %add_convert_fusion.1), channel_id=1, source_target_pairs={{0,16},{1,17},{2,18},{3,19},{4,20},{5,21},{6,22},{7,23},{8,24},{9,... | collective-permute-start | bytes 147464 | tf_op jit(solution)/shard_map/ppermute | solution.py:394
  132.8 2.1 %collective-permute-done.13 = bf16[48,512]{1,0:T(8,128)(2,1)S(1)} collective-permute-done((bf16[48,512]{1,0:T(8,128)(2,1)S(1)}, bf16[48,512]{1,0:T(8,128)(2,1)S(1)}, u32[]{:S(2)}, u32[]{:S(2)}) %collective-permute-start.13) | collective-permute-done | bytes 49184 | tf_op jit(solution)/shard_map/ppermute | solution.py:394
  134.9 2.0 %collective-permute-done.12 = bf16[48,512]{1,0:T(8,128)(2,1)S(1)} collective-permute-done((bf16[48,512]{1,0:T(8,128)(2,1)S(1)}, bf16[48,512]{1,0:T(8,128)(2,1)S(1)}, u32[]{:S(2)}, u32[]{:S(2)}) %collective-permute-start.12) | collective-permute-done | bytes 49184 | tf_op jit(solution)/shard_map/ppermute | solution.py:394
  137.1 6.4 %collective-permute-start.15 = (bf16[48,512]{1,0:T(8,128)(2,1)S(1)}, bf16[48,512]{1,0:T(8,128)(2,1)S(1)}, u32[]{:S(2)}, u32[]{:S(2)}) collective-permute-start(bf16[48,512]{1,0:T(8,128)(2,1)S(1)} %add_convert_fusion.refs_1_), channel_id=1, source_target_pairs={{0,4},{1,5},{2,6},{3,7},{4,0},{5,1},{6,2},{7,3},{8,12},{9,13},{10,... | collective-permute-start | bytes 147464 | tf_op jit(solution)/shard_map/ppermute | solution.py:394
  143.5 3.1 %own_step.3.refs_0_ = bf16[64,512]{1,0:T(8,128)(2,1)S(1)} custom-call(s32[16,25]{1,0:T(8,128)S(1)} %maximum_convert_fusion.pos_ref, f32[2,256,256]{2,1,0:T(8,128)S(1)} %get-tuple-element.24.probe_ref, f32[64,512]{1,0:T(8,128)S(1)} %get-tuple-element.26.own_ref, bf16[64,512]{1,0:T(8,128)(2,1)S(1)} %collective-permute-done.10.up_ref), custom_call_target="tpu_custom_call" | custom-call | tf_op jit(solution)/shard_map/own_step/pallas_call | solution.py:318
  146.8 16.3 %all_to_all.23.recv_ref = bf16[8,112,512]{2,1,0:T(8,128)(2,1)S(1)} all-to-all(bf16[8,112,512]{2,1,0:T(8,128)(2,1)S(1)} %spread.3), channel_id=1, replica_groups=mesh['scan'=8,'tile'=32] {'scan'}, dimensions={0} | all-to-all | bytes 1835008 | tf_op jit(solution)/shard_map/all_to_all | solution.py:407
  163.0 1.4 final.1
  (42 shorter events, 1.0 us)
Async XLA Ops:
  0.6 13.4 %copy-start = (f32[2,256,512]{2,1,0:T(8,128)S(1)}, f32[2,256,512]{2,1,0:T(8,128)}, u32[]{:S(2)}) copy-start(f32[2,256,512]{2,1,0:T(8,128)} %obj_ref.3) | copy-start | bytes 3145732
  0.6 7.4 %copy-start.4 = (s32[1,1,12,2]{2,3,1,0:T(2,128)S(1)}, s32[1,1,12,2]{2,3,1,0:T(2,128)}, u32[]{:S(2)}) copy-start(s32[1,1,12,2]{2,3,1,0:T(2,128)} %param.9) | copy-start | bytes 292
  0.7 13.4 %copy-start.1 = (f32[2,256,256]{2,1,0:T(8,128)S(1)}, f32[2,256,256]{2,1,0:T(8,128)}, u32[]{:S(2)}) copy-start(f32[2,256,256]{2,1,0:T(8,128)} %probe_ref.5) | copy-start | bytes 1572868
  2.1 12.0 %collective-permute-start = (bf16[2,256,512]{2,1,0:T(8,128)(2,1)S(1)}, bf16[2,256,512]{2,1,0:T(8,128)(2,1)S(1)}, u32[]{:S(2)}, u32[]{:S(2)}) collective-permute-start(bf16[2,256,512]{2,1,0:T(8,128)(2,1)S(1)} %convert_element_type.62), channel_id=1, source_target_pairs={{0,31},{1,0},{2,1},{3,2},{4,3},{5,4},{6,5},{7,6},{8,7},{9,8},{10,9... | collective-permute-start | bytes 1572872 | tf_op jit(solution)/shard_map/ppermute | solution.py:390
  8.2 1.4 copy-start.2
  9.6 1.0 copy-start.3
  45.8 1.3 collective-permute-start.3
  45.9 10.5 %collective-permute-start.1 = (bf16[80,512]{1,0:T(8,128)(2,1)S(1)}, bf16[80,512]{1,0:T(8,128)(2,1)S(1)}, u32[]{:S(2)}, u32[]{:S(2)}) collective-permute-start(bf16[80,512]{1,0:T(8,128)(2,1)S(1)} %get-tuple-element.19), channel_id=1, source_target_pairs={{0,1},{1,2},{2,3},{3,4},{4,5},{5,6},{6,7},{7,8},{8,9},{9,10},{10,1... | collective-permute-start | bytes 245768 | tf_op jit(solution)/shard_map/ppermute | solution.py:390
  47.2 13.4 %collective-permute-start.6 = (bf16[48,512]{1,0:T(8,128)(2,1)S(1)}, bf16[48,512]{1,0:T(8,128)(2,1)S(1)}, u32[]{:S(2)}, u32[]{:S(2)}) collective-permute-start(bf16[48,512]{1,0:T(8,128)(2,1)S(1)} %add_convert_fusion.3), channel_id=1, source_target_pairs={{0,18},{1,19},{2,16},{3,17},{4,22},{5,23},{6,20},{7,21},{8,26},{9,... | collective-permute-start | bytes 147464 | tf_op jit(solution)/shard_map/ppermute | solution.py:394
  47.3 13.3 %collective-permute-start.5 = (bf16[48,512]{1,0:T(8,128)(2,1)S(1)}, bf16[48,512]{1,0:T(8,128)(2,1)S(1)}, u32[]{:S(2)}, u32[]{:S(2)}) collective-permute-start(bf16[48,512]{1,0:T(8,128)(2,1)S(1)} %add_convert_fusion.3), channel_id=1, source_target_pairs={{0,16},{1,17},{2,18},{3,19},{4,20},{5,21},{6,22},{7,23},{8,24},{9,... | collective-permute-start | bytes 147464 | tf_op jit(solution)/shard_map/ppermute | solution.py:394
  53.8 6.8 %collective-permute-start.4 = (bf16[48,512]{1,0:T(8,128)(2,1)S(1)}, bf16[48,512]{1,0:T(8,128)(2,1)S(1)}, u32[]{:S(2)}, u32[]{:S(2)}) collective-permute-start(bf16[48,512]{1,0:T(8,128)(2,1)S(1)} %add_convert_fusion.3), channel_id=1, source_target_pairs={{0,2},{1,3},{2,0},{3,1},{4,6},{5,7},{6,4},{7,5},{8,10},{9,11},{10,... | collective-permute-start | bytes 147464 | tf_op jit(solution)/shard_map/ppermute | solution.py:394
  59.6 10.2 %collective-permute-start.2 = (bf16[64,512]{1,0:T(8,128)(2,1)S(1)}, bf16[64,512]{1,0:T(8,128)(2,1)S(1)}, u32[]{:S(2)}, u32[]{:S(2)}) collective-permute-start(bf16[64,512]{1,0:T(8,128)(2,1)S(1)} %own_step.2.refs_0_), channel_id=1, source_target_pairs={{0,31},{1,0},{2,1},{3,2},{4,3},{5,4},{6,5},{7,6},{8,7},{9,8},{10,9... | collective-permute-start | bytes 196616 | tf_op jit(solution)/shard_map/ppermute | solution.py:390
  60.6 6.6 %collective-permute-start.9 = (bf16[48,512]{1,0:T(8,128)(2,1)S(1)}, bf16[48,512]{1,0:T(8,128)(2,1)S(1)}, u32[]{:S(2)}, u32[]{:S(2)}) collective-permute-start(bf16[48,512]{1,0:T(8,128)(2,1)S(1)} %add_convert_fusion.2.refs_2_), channel_id=1, source_target_pairs={{0,12},{1,13},{2,14},{3,15},{4,8},{5,9},{6,10},{7,11},{8,4},{9,5},... | collective-permute-start | bytes 147464 | tf_op jit(solution)/shard_map/ppermute | solution.py:394
  61.6 8.2 %collective-permute-start.8 = (bf16[48,512]{1,0:T(8,128)(2,1)S(1)}, bf16[48,512]{1,0:T(8,128)(2,1)S(1)}, u32[]{:S(2)}, u32[]{:S(2)}) collective-permute-start(bf16[48,512]{1,0:T(8,128)(2,1)S(1)} %add_convert_fusion.2.refs_2_), channel_id=1, source_target_pairs={{0,8},{1,9},{2,10},{3,11},{4,12},{5,13},{6,14},{7,15},{8,0},{9,1},... | collective-permute-start | bytes 147464 | tf_op jit(solution)/shard_map/ppermute | solution.py:394
  63.5 6.2 %collective-permute-start.7 = (bf16[48,512]{1,0:T(8,128)(2,1)S(1)}, bf16[48,512]{1,0:T(8,128)(2,1)S(1)}, u32[]{:S(2)}, u32[]{:S(2)}) collective-permute-start(bf16[48,512]{1,0:T(8,128)(2,1)S(1)} %add_convert_fusion.2.refs_2_), channel_id=1, source_target_pairs={{0,4},{1,5},{2,6},{3,7},{4,0},{5,1},{6,2},{7,3},{8,12},{9,13},{10,... | collective-permute-start | bytes 147464 | tf_op jit(solution)/shard_map/ppermute | solution.py:394
  122.5 1.3 collective-permute-start.11
  123.8 9.0 %collective-permute-start.14 = (bf16[48,512]{1,0:T(8,128)(2,1)S(1)}, bf16[48,512]{1,0:T(8,128)(2,1)S(1)}, u32[]{:S(2)}, u32[]{:S(2)}) collective-permute-start(bf16[48,512]{1,0:T(8,128)(2,1)S(1)} %add_convert_fusion.1), channel_id=1, source_target_pairs={{0,18},{1,19},{2,16},{3,17},{4,22},{5,23},{6,20},{7,21},{8,26},{9,... | collective-permute-start | bytes 147464 | tf_op jit(solution)/shard_map/ppermute | solution.py:394
  123.9 10.9 %collective-permute-start.13 = (bf16[48,512]{1,0:T(8,128)(2,1)S(1)}, bf16[48,512]{1,0:T(8,128)(2,1)S(1)}, u32[]{:S(2)}, u32[]{:S(2)}) collective-permute-start(bf16[48,512]{1,0:T(8,128)(2,1)S(1)} %add_convert_fusion.1), channel_id=1, source_target_pairs={{0,16},{1,17},{2,18},{3,19},{4,20},{5,21},{6,22},{7,23},{8,24},{9,... | collective-permute-start | bytes 147464 | tf_op jit(solution)/shard_map/ppermute | solution.py:394
  132.8 4.1 %collective-permute-start.12 = (bf16[48,512]{1,0:T(8,128)(2,1)S(1)}, bf16[48,512]{1,0:T(8,128)(2,1)S(1)}, u32[]{:S(2)}, u32[]{:S(2)}) collective-permute-start(bf16[48,512]{1,0:T(8,128)(2,1)S(1)} %add_convert_fusion.1), channel_id=1, source_target_pairs={{0,2},{1,3},{2,0},{3,1},{4,6},{5,7},{6,4},{7,5},{8,10},{9,11},{10,... | collective-permute-start | bytes 147464 | tf_op jit(solution)/shard_map/ppermute | solution.py:394
  132.8 10.7 %collective-permute-start.10 = (bf16[64,512]{1,0:T(8,128)(2,1)S(1)}, bf16[64,512]{1,0:T(8,128)(2,1)S(1)}, u32[]{:S(2)}, u32[]{:S(2)}) collective-permute-start(bf16[64,512]{1,0:T(8,128)(2,1)S(1)} %get-tuple-element.27), channel_id=1, source_target_pairs={{0,1},{1,2},{2,3},{3,4},{4,5},{5,6},{6,7},{7,8},{8,9},{9,10},{10,1... | collective-permute-start | bytes 196616 | tf_op jit(solution)/shard_map/ppermute | solution.py:390
  136.9 9.7 %collective-permute-start.17 = (bf16[48,512]{1,0:T(8,128)(2,1)S(1)}, bf16[48,512]{1,0:T(8,128)(2,1)S(1)}, u32[]{:S(2)}, u32[]{:S(2)}) collective-permute-start(bf16[48,512]{1,0:T(8,128)(2,1)S(1)} %add_convert_fusion.refs_1_), channel_id=1, source_target_pairs={{0,12},{1,13},{2,14},{3,15},{4,8},{5,9},{6,10},{7,11},{8,4},{9,5},... | collective-permute-start | bytes 147464 | tf_op jit(solution)/shard_map/ppermute | solution.py:394
  137.0 9.6 %collective-permute-start.16 = (bf16[48,512]{1,0:T(8,128)(2,1)S(1)}, bf16[48,512]{1,0:T(8,128)(2,1)S(1)}, u32[]{:S(2)}, u32[]{:S(2)}) collective-permute-start(bf16[48,512]{1,0:T(8,128)(2,1)S(1)} %add_convert_fusion.refs_1_), channel_id=1, source_target_pairs={{0,8},{1,9},{2,10},{3,11},{4,12},{5,13},{6,14},{7,15},{8,0},{9,1},... | collective-permute-start | bytes 147464 | tf_op jit(solution)/shard_map/ppermute | solution.py:394
  137.1 9.5 %collective-permute-start.15 = (bf16[48,512]{1,0:T(8,128)(2,1)S(1)}, bf16[48,512]{1,0:T(8,128)(2,1)S(1)}, u32[]{:S(2)}, u32[]{:S(2)}) collective-permute-start(bf16[48,512]{1,0:T(8,128)(2,1)S(1)} %add_convert_fusion.refs_1_), channel_id=1, source_target_pairs={{0,4},{1,5},{2,6},{3,7},{4,0},{5,1},{6,2},{7,3},{8,12},{9,13},{10,... | collective-permute-start | bytes 147464 | tf_op jit(solution)/shard_map/ppermute | solution.py:394
